TPU v7x, 32 devices: a whole 2x2x4 slice. The times are simulated.
32 devices in a mesh: vin: 8 (over z, core), vout: 2 (over x), cell: 2 (over y).
Axes of the slice: x: 2, y: 2, z: 4, core: 2. Of those that a mesh axis runs over, the one named last changes fastest.
Arguments:
- distribution: bfloat16 [8, 13824, 4, 128], P('vout', 'vin', 'cell'), may hold values from -6 to 6
- collision: bfloat16 [13824, 13824], P('vout', 'vin'), may hold values from -1 to 3
- speeds: float32 [3, 13824], P(None, 'vout'), may hold values from 0.05 to 0.3
- directions: int32 [3, 13824], P(None, 'vout'), may hold values from 0 to 1
- cell_flags: int32 [8, 4, 128], P('vin', 'cell'), may hold values 0 or 1
Outputs:
- updated: bfloat16 [8, 13824, 4, 128], P('vin', 'vout', 'cell')
Inputs may be any that keep to these rules, and one draw needn't show every extreme that they name: `directions`: 1 means the component is positive, 0 negative. `cell_flags`: 1 marks a solid cell, where nothing is transported.
All inputs are finite; a program needn't handle non-finite values. No bound on the sum of `cell_flags` on one device may be relied on, other than what follows from the above.
Results may differ from a plain program's by a relative error of at most 0.023.
Values may be sent and summed in bfloat16 or wider, within the bound.
A program may use at most 128 MiB of HBM per device.

v0:
```python
import jax
import jax.numpy as jnp
from jax import lax
from jax.sharding import PartitionSpec as P

CHUNKS = 3
CORES = 2


def from_lower(values, axis):
    ends = lax.axis_size(axis) - 1
    return lax.ppermute(values, axis, [(i, i + 1) for i in range(ends)])


def from_higher(values, axis):
    ends = lax.axis_size(axis) - 1
    return lax.ppermute(values, axis, [(i + 1, i) for i in range(ends)])


def hop(values, axis, pairs):
    return lax.ppermute(values, axis, pairs)


def core_pairs(axis):
    return [(i, i + 1 - 2 * (i % CORES)) for i in range(lax.axis_size(axis))]


def scatter_line(own, axis):
    chips = lax.axis_size(axis) // CORES
    chip = lax.axis_index(axis) // CORES
    total = lax.dynamic_index_in_dim(own, chip, 0, keepdims=False).astype(jnp.float32)
    up = down = None
    for step in range(chips - 1):
        target = jnp.clip(chips - 1 - step + chip, 0, chips - 1)
        lower = jnp.clip(step - (chips - 1 - chip), 0, chips - 1)
        send_up = lax.dynamic_index_in_dim(own, target, 0, keepdims=False)
        send_down = lax.dynamic_index_in_dim(own, lower, 0, keepdims=False)
        if step:
            send_up = (send_up.astype(jnp.float32) + up.astype(jnp.float32)).astype(own.dtype)
            send_down = (send_down.astype(jnp.float32) + down.astype(jnp.float32)).astype(own.dtype)
        rising, falling = [], []
        for at in range(step + 1):
            mirror = chips - 1 - at
            for core in range(CORES):
                rising.append((at * CORES + core, (at + 1) * CORES + core))
                falling.append((mirror * CORES + core, (mirror - 1) * CORES + core))
        up = hop(send_up, axis, rising)
        down = hop(send_down, axis, falling)
    if up is not None:
        total = total + up.astype(jnp.float32) + down.astype(jnp.float32)
    return total.astype(own.dtype)


def shifted(values, step):
    edge = jnp.zeros_like(values[..., :1])
    if step > 0:
        return jnp.concatenate([edge, values[..., :-1]], axis=-1)
    return jnp.concatenate([values[..., 1:], edge], axis=-1)


def transport(center, neighbours, speeds, positive, fluid):
    middle = center.astype(jnp.float32)
    flux = jnp.zeros_like(middle)
    for component, (low, high) in enumerate(neighbours):
        upstream = jnp.where(positive[component][:, None, None], low, high).astype(jnp.float32)
        flux = flux + speeds[component][:, None, None] * (middle - upstream)
    return (middle - fluid[None] * flux).astype(jnp.bfloat16)


def on_device(distribution, collision, speeds, directions, cell_flags):
    velocities = collision.shape[0]
    chunk = velocities // CHUNKS
    planes = lax.all_gather(distribution, "vout", axis=0, tiled=True)
    planes = planes.reshape((planes.shape[0] // CORES, CORES) + planes.shape[1:])
    core = lax.rem(lax.axis_index("vin"), CORES)
    mine = lax.dynamic_index_in_dim(planes, core, 1, keepdims=False)
    theirs = lax.dynamic_index_in_dim(planes, 1 - core, 1, keepdims=False)
    fluid = (1 - cell_flags[0]).astype(jnp.float32)
    outs = []
    for part in range(CHUNKS):
        own = slice(part * chunk, (part + 1) * chunk)
        block = collision[own]
        spec = "vu,zuyx->zvyx"
        away = jnp.einsum(spec, block, theirs, preferred_element_type=jnp.float32)
        near = jnp.einsum(spec, block, mine, preferred_element_type=jnp.float32)
        got = hop(away.astype(jnp.bfloat16), "vin", core_pairs("vin"))
        both = (near + got.astype(jnp.float32)).astype(jnp.bfloat16)
        cells = scatter_line(both, "vin")
        before = from_lower(cells[:, -1:], "cell")
        after = from_higher(cells[:, :1], "cell")
        neighbours = (
            (shifted(cells, 1), shifted(cells, -1)),
            (
                jnp.concatenate([before, cells[:, :-1]], axis=1),
                jnp.concatenate([cells[:, 1:], after], axis=1),
            ),
            (from_lower(cells, "vin"), from_higher(cells, "vin")),
        )
        outs.append(transport(cells, neighbours, speeds[:, own], directions[:, own] == 1, fluid))
    return jnp.concatenate(outs, axis=0)[None]


def solution(mesh):
    return jax.shard_map(
        on_device,
        mesh=mesh,
        in_specs=(
            P("vout", "vin", "cell", None),
            P("vout", "vin"),
            P(None, "vout"),
            P(None, "vout"),
            P("vin", "cell", None),
        ),
        out_specs=P("vin", "vout", "cell", None),
        check_vma=False,
    )
```

profile of v0, /device:TPU:8, one launch (start us, length us, event | category | flops | bytes accessed | tf_op | source)
XLA Modules:
  0.0 504.8 jit_solution(819726647843778147)
XLA Ops:
  6.5 4.2 copy.9
  10.8 90.5 %all-gather.2.cloned.1.call-done = bf16[8,1728,2,128]{3,1,2,0:T(8,128)(2,1)} async-done(((bf16[4,1728,2,128]{3,1,2,0:T(8,128)(2,1)}), bf16[8,1728,2,128]{3,1,2,0:T(8,128)(2,1)}) %all-gather.2.cloned.1.call-update) | async-done | bytes 7077904 | tf_op jit(solution)/shard_map/all_gather | solution.py:73
  101.4 14.5 %fusion.42 = bf16[4,2304,2,128]{1,3,2,0:T(8,128)(2,1)} fusion(bf16[6912,1728]{0,1:T(8,128)(2,1)} %param.6, bf16[4,2,1728,2,128]{4,2,3,1,0:T(8,128)(2,1)} %bitcast.137, s32[]{:T(128)S(6)} %select_n.67), kind=kOutput, calls=%fused_computation.29 | convolution fusion | flops 8156086272 | bytes 16220164 | tf_op jit(solution)/shard_map/vu,zuyx->zvyx/dot_general | solution.py:84
  115.9 13.7 %fusion.39 = bf16[4,2304,2,128]{1,3,2,0:T(8,128)(2,1)} fusion(bf16[6912,1728]{0,1:T(8,128)(2,1)} %param.6, bf16[4,2,1728,2,128]{4,2,3,1,0:T(8,128)(2,1)S(1)} %bitcast.141, s32[]{:T(128)S(6)} %select_n.67), kind=kOutput, calls=%fused_computation.28 | convolution fusion | flops 8156086272 | bytes 16220164 | tf_op jit(solution)/shard_map/vu,zuyx->zvyx/dot_general | solution.py:84
  130.1 13.9 %fusion.36 = bf16[4,2304,2,128]{1,3,2,0:T(8,128)(2,1)} fusion(bf16[6912,1728]{0,1:T(8,128)(2,1)} %param.6, bf16[4,2,1728,2,128]{4,2,3,1,0:T(8,128)(2,1)S(1)} %bitcast.142, s32[]{:T(128)S(6)} %select_n.67), kind=kOutput, calls=%fused_computation.27 | convolution fusion | flops 8156086272 | bytes 16220164 | tf_op jit(solution)/shard_map/vu,zuyx->zvyx/dot_general | solution.py:84
  144.7 13.6 %fusion.2 = bf16[4,2304,2,128]{1,3,2,0:T(8,128)(2,1)S(1)} fusion(bf16[4,2304,2,128]{1,3,2,0:T(8,128)(2,1)} %collective-permute-done, bf16[6912,1728]{0,1:T(8,128)(2,1)} %param.6, bf16[4,2,1728,2,128]{4,2,3,1,0:T(8,128)(2,1)} %bitcast.138, s32[]{:T(128)S(6)} %select_n.66), kind=kOutput, calls=%fused_computation.5 | convolution fusion | flops 8160804864 | bytes 20938756 | tf_op jit(solution)/shard_map/vu,zuyx->zvyx/dot_general | solution.py:85
  161.4 13.8 %fusion.1 = bf16[4,2304,2,128]{1,3,2,0:T(8,128)(2,1)S(1)} fusion(bf16[4,2304,2,128]{1,3,2,0:T(8,128)(2,1)} %collective-permute-done.11, bf16[6912,1728]{0,1:T(8,128)(2,1)} %param.6, bf16[4,2,1728,2,128]{4,2,3,1,0:T(8,128)(2,1)} %bitcast.139, s32[]{:T(128)S(6)} %select_n.66), kind=kOutput, calls=%fused_computation.3 | convolution fusion | flops 8160804864 | bytes 20938756 | tf_op jit(solution)/shard_map/vu,zuyx->zvyx/dot_general | solution.py:85
  178.3 13.6 %fusion = bf16[4,2304,2,128]{1,3,2,0:T(8,128)(2,1)S(1)} fusion(bf16[4,2304,2,128]{1,3,2,0:T(8,128)(2,1)} %collective-permute-done.22, bf16[6912,1728]{0,1:T(8,128)(2,1)} %param.6, bf16[4,2,1728,2,128]{4,2,3,1,0:T(8,128)(2,1)} %bitcast.140, s32[]{:T(128)S(6)} %select_n.66), kind=kOutput, calls=%fused_computation.1 | convolution fusion | flops 8160804864 | bytes 20938756 | tf_op jit(solution)/shard_map/vu,zuyx->zvyx/dot_general | solution.py:85
  194.4 20.1 %collective-permute-done.12 = bf16[2304,2,128]{0,2,1:T(8,128)(2,1)} collective-permute-done((bf16[2304,2,128]{0,2,1:T(8,128)(2,1)S(1)}, bf16[2304,2,128]{0,2,1:T(8,128)(2,1)}, u32[]{:S(2)}, u32[]{:S(2)}) %collective-permute-start.12) | collective-permute-done | bytes 1179680 | tf_op jit(solution)/shard_map/ppermute | solution.py:21
  218.0 21.7 %collective-permute-done.23 = bf16[2304,2,128]{0,2,1:T(8,128)(2,1)S(1)} collective-permute-done((bf16[2304,2,128]{0,2,1:T(8,128)(2,1)S(1)}, bf16[2304,2,128]{0,2,1:T(8,128)(2,1)S(1)}, u32[]{:S(2)}, u32[]{:S(2)}) %collective-permute-start.23) | collective-permute-done | bytes 1179680 | tf_op jit(solution)/shard_map/ppermute | solution.py:21
  243.8 21.1 %collective-permute-done.2 = bf16[2304,2,128]{0,2,1:T(8,128)(2,1)S(1)} collective-permute-done((bf16[2304,2,128]{0,2,1:T(8,128)(2,1)S(1)}, bf16[2304,2,128]{0,2,1:T(8,128)(2,1)S(1)}, u32[]{:S(2)}, u32[]{:S(2)}) %collective-permute-start.2) | collective-permute-done | bytes 1179680 | tf_op jit(solution)/shard_map/ppermute | solution.py:21
  268.1 4.8 collective-permute-start.3
  272.9 17.3 %collective-permute-done.13 = bf16[2304,2,128]{0,2,1:T(8,128)(2,1)S(1)} collective-permute-done((bf16[2304,2,128]{0,2,1:T(8,128)(2,1)S(1)}, bf16[2304,2,128]{0,2,1:T(8,128)(2,1)S(1)}, u32[]{:S(2)}, u32[]{:S(2)}) %collective-permute-start.13) | collective-permute-done | bytes 1179680 | tf_op jit(solution)/shard_map/ppermute | solution.py:21
  293.4 4.6 collective-permute-start.14
  297.9 17.5 %collective-permute-done.24 = bf16[2304,2,128]{0,2,1:T(8,128)(2,1)S(1)} collective-permute-done((bf16[2304,2,128]{0,2,1:T(8,128)(2,1)S(1)}, bf16[2304,2,128]{0,2,1:T(8,128)(2,1)S(1)}, u32[]{:S(2)}, u32[]{:S(2)}) %collective-permute-start.24) | collective-permute-done | bytes 1179680 | tf_op jit(solution)/shard_map/ppermute | solution.py:21
  317.4 4.6 collective-permute-start.25
  324.6 23.0 %collective-permute-done.27 = bf16[2304,2,128]{0,2,1:T(8,128)(2,1)S(1)} collective-permute-done((bf16[2304,2,128]{0,2,1:T(8,128)(2,1)S(1)}, bf16[2304,2,128]{0,2,1:T(8,128)(2,1)S(1)}, u32[]{:S(2)}, u32[]{:S(2)}) %collective-permute-start.27) | collective-permute-done | bytes 1179680 | tf_op jit(solution)/shard_map/ppermute | solution.py:21
  351.8 21.1 %collective-permute-done.6 = bf16[2304,2,128]{0,2,1:T(8,128)(2,1)S(1)} collective-permute-done((bf16[2304,2,128]{0,2,1:T(8,128)(2,1)S(1)}, bf16[2304,2,128]{0,2,1:T(8,128)(2,1)S(1)}, u32[]{:S(2)}, u32[]{:S(2)}) %collective-permute-start.6) | collective-permute-done | bytes 1179680 | tf_op jit(solution)/shard_map/ppermute | solution.py:21
  375.6 2.4 collective-permute-start.9
  378.0 20.2 %collective-permute-done.17 = bf16[2304,2,128]{0,2,1:T(8,128)(2,1)S(1)} collective-permute-done((bf16[2304,2,128]{0,2,1:T(8,128)(2,1)S(1)}, bf16[2304,2,128]{0,2,1:T(8,128)(2,1)S(1)}, u32[]{:S(2)}, u32[]{:S(2)}) %collective-permute-start.17) | collective-permute-done | bytes 1179680 | tf_op jit(solution)/shard_map/ppermute | solution.py:21
  400.9 3.4 collective-permute-start.7
  404.4 17.9 %collective-permute-done.28 = bf16[2304,2,128]{0,2,1:T(8,128)(2,1)S(1)} collective-permute-done((bf16[2304,2,128]{0,2,1:T(8,128)(2,1)S(1)}, bf16[2304,2,128]{0,2,1:T(8,128)(2,1)S(1)}, u32[]{:S(2)}, u32[]{:S(2)}) %collective-permute-start.28) | collective-permute-done | bytes 1179680 | tf_op jit(solution)/shard_map/ppermute | solution.py:21
  426.3 12.0 %collective-permute-done.8 = bf16[2304,1,128]{0,2,1:T(8,128)(2,1)S(1)} collective-permute-done((bf16[2304,1,128]{0,2,1:T(8,128)(2,1)S(1)}, bf16[2304,1,128]{0,2,1:T(8,128)(2,1)S(1)}, u32[]{:S(2)}, u32[]{:S(2)}) %collective-permute-start.8) | collective-permute-done | bytes 589856 | tf_op jit(solution)/shard_map/ppermute | solution.py:17
  439.8 10.7 %collective-permute-done.18 = bf16[2304,1,128]{0,2,1:T(8,128)(2,1)S(1)} collective-permute-done((bf16[2304,1,128]{0,2,1:T(8,128)(2,1)S(1)}, bf16[2304,1,128]{0,2,1:T(8,128)(2,1)S(1)}, u32[]{:S(2)}, u32[]{:S(2)}) %collective-permute-start.18) | collective-permute-done | bytes 589856 | tf_op jit(solution)/shard_map/ppermute | solution.py:12
  452.4 3.6 collective-permute-start.32
  457.4 2.2 fusion.63
  459.6 12.5 %collective-permute-done.19 = bf16[2304,1,128]{0,2,1:T(8,128)(2,1)S(1)} collective-permute-done((bf16[2304,1,128]{0,2,1:T(8,128)(2,1)S(1)}, bf16[2304,1,128]{0,2,1:T(8,128)(2,1)S(1)}, u32[]{:S(2)}, u32[]{:S(2)}) %collective-permute-start.19) | collective-permute-done | bytes 589856 | tf_op jit(solution)/shard_map/ppermute | solution.py:17
  474.9 2.2 fusion.70
  477.1 7.3 %collective-permute-done.29 = bf16[2304,1,128]{0,2,1:T(8,128)(2,1)S(1)} collective-permute-done((bf16[2304,1,128]{0,2,1:T(8,128)(2,1)S(1)}, bf16[2304,1,128]{0,2,1:T(8,128)(2,1)S(1)}, u32[]{:S(2)}, u32[]{:S(2)}) %collective-permute-start.29) | collective-permute-done | bytes 589856 | tf_op jit(solution)/shard_map/ppermute | solution.py:12
  484.4 4.2 collective-permute-done.30
  488.5 2.2 fusion.77
  491.0 6.5 %copy.12 = bf16[1,6912,2,128]{3,2,1,0:T(2,128)(2,1)} copy(bf16[1,6912,2,128]{1,3,2,0:T(8,128)(2,1)S(1)} %maximum_bitcast_fusion) | data formatting | bytes 7077888 | tf_op jit(solution)/shard_map/broadcast_in_dim | solution.py:100
  (84 shorter events, 49.6 us)
Async XLA Ops:
  6.5 94.8 %all-gather.2.cloned.1.call-start = ((), (), s32[]{:S(2)}) async-start(), calls=%async_computation | async-start | bytes 10616832 | tf_op jit(solution)/shard_map/all_gather | solution.py:73
  115.8 28.8 %collective-permute-start = (bf16[4,2304,2,128]{1,3,2,0:T(8,128)(2,1)}, bf16[4,2304,2,128]{1,3,2,0:T(8,128)(2,1)}, u32[]{:S(2)}, u32[]{:S(2)}) collective-permute-start(bf16[4,2304,2,128]{1,3,2,0:T(8,128)(2,1)} %fusion.42), channel_id=1, source_target_pairs={{0,4},{4,0},{8,12},{12,8},{16,20},{20,16},{24,28},{28,24},{1,5},{5... | collective-permute-start | bytes 14155784 | tf_op jit(solution)/shard_map/ppermute | solution.py:21
  129.6 31.8 %collective-permute-start.11 = (bf16[4,2304,2,128]{1,3,2,0:T(8,128)(2,1)}, bf16[4,2304,2,128]{1,3,2,0:T(8,128)(2,1)}, u32[]{:S(2)}, u32[]{:S(2)}) collective-permute-start(bf16[4,2304,2,128]{1,3,2,0:T(8,128)(2,1)} %fusion.39), channel_id=1, source_target_pairs={{0,4},{4,0},{8,12},{12,8},{16,20},{20,16},{24,28},{28,24},{1,5},{5... | collective-permute-start | bytes 14155784 | tf_op jit(solution)/shard_map/ppermute | solution.py:21
  144.0 34.4 %collective-permute-start.22 = (bf16[4,2304,2,128]{1,3,2,0:T(8,128)(2,1)}, bf16[4,2304,2,128]{1,3,2,0:T(8,128)(2,1)}, u32[]{:S(2)}, u32[]{:S(2)}) collective-permute-start(bf16[4,2304,2,128]{1,3,2,0:T(8,128)(2,1)} %fusion.36), channel_id=1, source_target_pairs={{0,4},{4,0},{8,12},{12,8},{16,20},{20,16},{24,28},{28,24},{1,5},{5... | collective-permute-start | bytes 14155784 | tf_op jit(solution)/shard_map/ppermute | solution.py:21
  158.4 35.0 %collective-permute-start.1 = (bf16[2304,2,128]{0,2,1:T(8,128)(2,1)S(1)}, bf16[2304,2,128]{0,2,1:T(8,128)(2,1)S(1)}, u32[]{:S(2)}, u32[]{:S(2)}) collective-permute-start(bf16[2304,2,128]{0,2,1:T(8,128)(2,1)S(1)} %get-tuple-element.25), channel_id=1, source_target_pairs={{0,8},{4,12},{1,9},{5,13},{2,10},{6,14},{3,11},{7,15}} | collective-permute-start | bytes 3538952 | tf_op jit(solution)/shard_map/ppermute | solution.py:21
  159.7 82.2 %collective-permute-start.4 = (bf16[2304,2,128]{0,2,1:T(8,128)(2,1)S(1)}, bf16[2304,2,128]{0,2,1:T(8,128)(2,1)}, u32[]{:S(2)}, u32[]{:S(2)}) collective-permute-start(bf16[2304,2,128]{0,2,1:T(8,128)(2,1)S(1)} %get-tuple-element.26), channel_id=1, source_target_pairs={{24,16},{28,20},{25,17},{29,21},{26,18},{30,22},{27,19},{31,23}} | collective-permute-start | bytes 3538952 | tf_op jit(solution)/shard_map/ppermute | solution.py:21
  175.3 39.1 %collective-permute-start.12 = (bf16[2304,2,128]{0,2,1:T(8,128)(2,1)S(1)}, bf16[2304,2,128]{0,2,1:T(8,128)(2,1)}, u32[]{:S(2)}, u32[]{:S(2)}) collective-permute-start(bf16[2304,2,128]{0,2,1:T(8,128)(2,1)S(1)} %get-tuple-element.29), channel_id=1, source_target_pairs={{0,8},{4,12},{1,9},{5,13},{2,10},{6,14},{3,11},{7,15}} | collective-permute-start | bytes 3538952 | tf_op jit(solution)/shard_map/ppermute | solution.py:21
  176.6 91.5 %collective-permute-start.15 = (bf16[2304,2,128]{0,2,1:T(8,128)(2,1)S(1)}, bf16[2304,2,128]{0,2,1:T(8,128)(2,1)}, u32[]{:S(2)}, u32[]{:S(2)}) collective-permute-start(bf16[2304,2,128]{0,2,1:T(8,128)(2,1)S(1)} %get-tuple-element.30), channel_id=1, source_target_pairs={{24,16},{28,20},{25,17},{29,21},{26,18},{30,22},{27,19},{31,23}} | collective-permute-start | bytes 3538952 | tf_op jit(solution)/shard_map/ppermute | solution.py:21
  192.1 47.6 %collective-permute-start.23 = (bf16[2304,2,128]{0,2,1:T(8,128)(2,1)S(1)}, bf16[2304,2,128]{0,2,1:T(8,128)(2,1)S(1)}, u32[]{:S(2)}, u32[]{:S(2)}) collective-permute-start(bf16[2304,2,128]{0,2,1:T(8,128)(2,1)S(1)} %get-tuple-element.33), channel_id=1, source_target_pairs={{0,8},{4,12},{1,9},{5,13},{2,10},{6,14},{3,11},{7,15}} | collective-permute-start | bytes 3538952 | tf_op jit(solution)/shard_map/ppermute | solution.py:21
  193.4 100.0 %collective-permute-start.26 = (bf16[2304,2,128]{0,2,1:T(8,128)(2,1)S(1)}, bf16[2304,2,128]{0,2,1:T(8,128)(2,1)S(1)}, u32[]{:S(2)}, u32[]{:S(2)}) collective-permute-start(bf16[2304,2,128]{0,2,1:T(8,128)(2,1)S(1)} %get-tuple-element.34), channel_id=1, source_target_pairs={{24,16},{28,20},{25,17},{29,21},{26,18},{30,22},{27,19},{31,23}} | collective-permute-start | bytes 3538952 | tf_op jit(solution)/shard_map/ppermute | solution.py:21
  214.5 50.5 %collective-permute-start.2 = (bf16[2304,2,128]{0,2,1:T(8,128)(2,1)S(1)}, bf16[2304,2,128]{0,2,1:T(8,128)(2,1)S(1)}, u32[]{:S(2)}, u32[]{:S(2)}) collective-permute-start(bf16[2304,2,128]{0,2,1:T(8,128)(2,1)S(1)} %fusion.92), channel_id=1, source_target_pairs={{0,8},{4,12},{8,16},{12,20},{1,9},{5,13},{9,17},{13,21},{2,10},{6,... | collective-permute-start | bytes 3538952 | tf_op jit(solution)/shard_map/ppermute | solution.py:21
  239.6 50.6 %collective-permute-start.13 = (bf16[2304,2,128]{0,2,1:T(8,128)(2,1)S(1)}, bf16[2304,2,128]{0,2,1:T(8,128)(2,1)S(1)}, u32[]{:S(2)}, u32[]{:S(2)}) collective-permute-start(bf16[2304,2,128]{0,2,1:T(8,128)(2,1)S(1)} %fusion.86), channel_id=1, source_target_pairs={{0,8},{4,12},{8,16},{12,20},{1,9},{5,13},{9,17},{13,21},{2,10},{6,... | collective-permute-start | bytes 3538952 | tf_op jit(solution)/shard_map/ppermute | solution.py:21
  241.9 73.6 %collective-permute-start.24 = (bf16[2304,2,128]{0,2,1:T(8,128)(2,1)S(1)}, bf16[2304,2,128]{0,2,1:T(8,128)(2,1)S(1)}, u32[]{:S(2)}, u32[]{:S(2)}) collective-permute-start(bf16[2304,2,128]{0,2,1:T(8,128)(2,1)S(1)} %fusion.80), channel_id=1, source_target_pairs={{0,8},{4,12},{8,16},{12,20},{1,9},{5,13},{9,17},{13,21},{2,10},{6,... | collective-permute-start | bytes 3538952 | tf_op jit(solution)/shard_map/ppermute | solution.py:21
  266.8 50.6 %collective-permute-start.5 = (bf16[2304,2,128]{0,2,1:T(8,128)(2,1)S(1)}, bf16[2304,2,128]{0,2,1:T(8,128)(2,1)S(1)}, u32[]{:S(2)}, u32[]{:S(2)}) collective-permute-start(bf16[2304,2,128]{0,2,1:T(8,128)(2,1)S(1)} %get-tuple-element.24), channel_id=1, source_target_pairs={{24,16},{28,20},{16,8},{20,12},{25,17},{29,21},{17,9},{21,13},{26,... | collective-permute-start | bytes 3538952 | tf_op jit(solution)/shard_map/ppermute | solution.py:21
  268.1 81.7 %collective-permute-start.3 = (bf16[2304,2,128]{0,2,1:T(8,128)(2,1)S(1)}, bf16[2304,2,128]{0,2,1:T(8,128)(2,1)S(1)}, u32[]{:S(2)}, u32[]{:S(2)}) collective-permute-start(bf16[2304,2,128]{0,2,1:T(8,128)(2,1)S(1)} %get-tuple-element.23), channel_id=1, source_target_pairs={{0,8},{4,12},{8,16},{12,20},{16,24},{20,28},{1,9},{5,13},{9,17},{1... | collective-permute-start | bytes 3538952 | tf_op jit(solution)/shard_map/ppermute | solution.py:21
  292.1 30.2 %collective-permute-start.16 = (bf16[2304,2,128]{0,2,1:T(8,128)(2,1)S(1)}, bf16[2304,2,128]{0,2,1:T(8,128)(2,1)S(1)}, u32[]{:S(2)}, u32[]{:S(2)}) collective-permute-start(bf16[2304,2,128]{0,2,1:T(8,128)(2,1)S(1)} %get-tuple-element.28), channel_id=1, source_target_pairs={{24,16},{28,20},{16,8},{20,12},{25,17},{29,21},{17,9},{21,13},{26,... | collective-permute-start | bytes 3538952 | tf_op jit(solution)/shard_map/ppermute | solution.py:21
  293.4 82.2 %collective-permute-start.14 = (bf16[2304,2,128]{0,2,1:T(8,128)(2,1)S(1)}, bf16[2304,2,128]{0,2,1:T(8,128)(2,1)S(1)}, u32[]{:S(2)}, u32[]{:S(2)}) collective-permute-start(bf16[2304,2,128]{0,2,1:T(8,128)(2,1)S(1)} %get-tuple-element.27), channel_id=1, source_target_pairs={{0,8},{4,12},{8,16},{12,20},{16,24},{20,28},{1,9},{5,13},{9,17},{1... | collective-permute-start | bytes 3538952 | tf_op jit(solution)/shard_map/ppermute | solution.py:21
  316.1 31.5 %collective-permute-start.27 = (bf16[2304,2,128]{0,2,1:T(8,128)(2,1)S(1)}, bf16[2304,2,128]{0,2,1:T(8,128)(2,1)S(1)}, u32[]{:S(2)}, u32[]{:S(2)}) collective-permute-start(bf16[2304,2,128]{0,2,1:T(8,128)(2,1)S(1)} %get-tuple-element.32), channel_id=1, source_target_pairs={{24,16},{28,20},{16,8},{20,12},{25,17},{29,21},{17,9},{21,13},{26,... | collective-permute-start | bytes 3538952 | tf_op jit(solution)/shard_map/ppermute | solution.py:21
  317.4 83.6 %collective-permute-start.25 = (bf16[2304,2,128]{0,2,1:T(8,128)(2,1)S(1)}, bf16[2304,2,128]{0,2,1:T(8,128)(2,1)S(1)}, u32[]{:S(2)}, u32[]{:S(2)}) collective-permute-start(bf16[2304,2,128]{0,2,1:T(8,128)(2,1)S(1)} %get-tuple-element.31), channel_id=1, source_target_pairs={{0,8},{4,12},{8,16},{12,20},{16,24},{20,28},{1,9},{5,13},{9,17},{1... | collective-permute-start | bytes 3538952 | tf_op jit(solution)/shard_map/ppermute | solution.py:21
  322.3 50.6 %collective-permute-start.6 = (bf16[2304,2,128]{0,2,1:T(8,128)(2,1)S(1)}, bf16[2304,2,128]{0,2,1:T(8,128)(2,1)S(1)}, u32[]{:S(2)}, u32[]{:S(2)}) collective-permute-start(bf16[2304,2,128]{0,2,1:T(8,128)(2,1)S(1)} %fusion.91), channel_id=1, source_target_pairs={{24,16},{28,20},{16,8},{20,12},{8,0},{12,4},{25,17},{29,21},{17,9}... | collective-permute-start | bytes 3538952 | tf_op jit(solution)/shard_map/ppermute | solution.py:21
  347.6 50.6 %collective-permute-start.17 = (bf16[2304,2,128]{0,2,1:T(8,128)(2,1)S(1)}, bf16[2304,2,128]{0,2,1:T(8,128)(2,1)S(1)}, u32[]{:S(2)}, u32[]{:S(2)}) collective-permute-start(bf16[2304,2,128]{0,2,1:T(8,128)(2,1)S(1)} %fusion.85), channel_id=1, source_target_pairs={{24,16},{28,20},{16,8},{20,12},{8,0},{12,4},{25,17},{29,21},{17,9}... | collective-permute-start | bytes 3538952 | tf_op jit(solution)/shard_map/ppermute | solution.py:21
  349.8 72.4 %collective-permute-start.28 = (bf16[2304,2,128]{0,2,1:T(8,128)(2,1)S(1)}, bf16[2304,2,128]{0,2,1:T(8,128)(2,1)S(1)}, u32[]{:S(2)}, u32[]{:S(2)}) collective-permute-start(bf16[2304,2,128]{0,2,1:T(8,128)(2,1)S(1)} %fusion.79), channel_id=1, source_target_pairs={{24,16},{28,20},{16,8},{20,12},{8,0},{12,4},{25,17},{29,21},{17,9}... | collective-permute-start | bytes 3538952 | tf_op jit(solution)/shard_map/ppermute | solution.py:21
  373.4 79.0 %collective-permute-start.10 = (bf16[2304,2,128]{0,2,1:T(8,128)(2,1)S(1)}, bf16[2304,2,128]{0,2,1:T(8,128)(2,1)S(1)}, u32[]{:S(2)}, u32[]{:S(2)}) collective-permute-start(bf16[2304,2,128]{0,2,1:T(8,128)(2,1)S(1)} %fusion.95), channel_id=1, source_target_pairs={{4,0},{8,4},{12,8},{16,12},{20,16},{24,20},{28,24},{5,1},{9,5},{13... | collective-permute-start | bytes 3538952 | tf_op jit(solution)/shard_map/ppermute | solution.py:17
  375.6 80.5 %collective-permute-start.9 = (bf16[2304,2,128]{0,2,1:T(8,128)(2,1)S(1)}, bf16[2304,2,128]{0,2,1:T(8,128)(2,1)S(1)}, u32[]{:S(2)}, u32[]{:S(2)}) collective-permute-start(bf16[2304,2,128]{0,2,1:T(8,128)(2,1)S(1)} %fusion.95), channel_id=1, source_target_pairs={{0,4},{4,8},{8,12},{12,16},{16,20},{20,24},{24,28},{1,5},{5,9},{9,... | collective-permute-start | bytes 3538952 | tf_op jit(solution)/shard_map/ppermute | solution.py:12
  398.6 74.9 %collective-permute-start.20 = (bf16[2304,2,128]{0,2,1:T(8,128)(2,1)S(1)}, bf16[2304,2,128]{0,2,1:T(8,128)(2,1)S(1)}, u32[]{:S(2)}, u32[]{:S(2)}) collective-permute-start(bf16[2304,2,128]{0,2,1:T(8,128)(2,1)S(1)} %fusion.89), channel_id=1, source_target_pairs={{0,4},{4,8},{8,12},{12,16},{16,20},{20,24},{24,28},{1,5},{5,9},{9,... | collective-permute-start | bytes 3538952 | tf_op jit(solution)/shard_map/ppermute | solution.py:12
  400.9 23.4 %collective-permute-start.7 = (bf16[2304,1,128]{0,2,1:T(8,128)(2,1)S(1)}, bf16[2304,1,128]{0,2,1:T(8,128)(2,1)S(1)}, u32[]{:S(2)}, u32[]{:S(2)}) collective-permute-start(bf16[2304,1,128]{0,2,1:T(8,128)(2,1)S(1)} %get-tuple-element.37), channel_id=1, source_target_pairs={{0,1},{2,3},{4,5},{6,7},{8,9},{10,11},{12,13},{14,15},{16,17},{18,... | collective-permute-start | bytes 1769480 | tf_op jit(solution)/shard_map/ppermute | solution.py:12
  422.2 16.0 %collective-permute-start.8 = (bf16[2304,1,128]{0,2,1:T(8,128)(2,1)S(1)}, bf16[2304,1,128]{0,2,1:T(8,128)(2,1)S(1)}, u32[]{:S(2)}, u32[]{:S(2)}) collective-permute-start(bf16[2304,1,128]{0,2,1:T(8,128)(2,1)S(1)} %get-tuple-element.38), channel_id=1, source_target_pairs={{1,0},{3,2},{5,4},{7,6},{9,8},{11,10},{13,12},{15,14},{17,16},{19,... | collective-permute-start | bytes 1769480 | tf_op jit(solution)/shard_map/ppermute | solution.py:17
  424.3 50.6 %collective-permute-start.21 = (bf16[2304,2,128]{0,2,1:T(8,128)(2,1)S(1)}, bf16[2304,2,128]{0,2,1:T(8,128)(2,1)S(1)}, u32[]{:S(2)}, u32[]{:S(2)}) collective-permute-start(bf16[2304,2,128]{0,2,1:T(8,128)(2,1)S(1)} %fusion.89), channel_id=1, source_target_pairs={{4,0},{8,4},{12,8},{16,12},{20,16},{24,20},{28,24},{5,1},{9,5},{13... | collective-permute-start | bytes 3538952 | tf_op jit(solution)/shard_map/ppermute | solution.py:17
  450.5 38.1 %collective-permute-start.31 = (bf16[2304,2,128]{0,2,1:T(8,128)(2,1)S(1)}, bf16[2304,2,128]{0,2,1:T(8,128)(2,1)S(1)}, u32[]{:S(2)}, u32[]{:S(2)}) collective-permute-start(bf16[2304,2,128]{0,2,1:T(8,128)(2,1)S(1)} %fusion.83), channel_id=1, source_target_pairs={{0,4},{4,8},{8,12},{12,16},{16,20},{20,24},{24,28},{1,5},{5,9},{9,... | collective-permute-start | bytes 3538952 | tf_op jit(solution)/shard_map/ppermute | solution.py:12
  452.4 36.1 %collective-permute-start.32 = (bf16[2304,2,128]{0,2,1:T(8,128)(2,1)S(1)}, bf16[2304,2,128]{0,2,1:T(8,128)(2,1)S(1)}, u32[]{:S(2)}, u32[]{:S(2)}) collective-permute-start(bf16[2304,2,128]{0,2,1:T(8,128)(2,1)S(1)} %fusion.83), channel_id=1, source_target_pairs={{4,0},{8,4},{12,8},{16,12},{20,16},{24,20},{28,24},{5,1},{9,5},{13... | collective-permute-start | bytes 3538952 | tf_op jit(solution)/shard_map/ppermute | solution.py:17
  456.1 16.0 %collective-permute-start.19 = (bf16[2304,1,128]{0,2,1:T(8,128)(2,1)S(1)}, bf16[2304,1,128]{0,2,1:T(8,128)(2,1)S(1)}, u32[]{:S(2)}, u32[]{:S(2)}) collective-permute-start(bf16[2304,1,128]{0,2,1:T(8,128)(2,1)S(1)} %get-tuple-element.42), channel_id=1, source_target_pairs={{1,0},{3,2},{5,4},{7,6},{9,8},{11,10},{13,12},{15,14},{17,16},{19,... | collective-permute-start | bytes 1769480 | tf_op jit(solution)/shard_map/ppermute | solution.py:17
  473.6 14.9 %collective-permute-start.30 = (bf16[2304,1,128]{0,2,1:T(8,128)(2,1)S(1)}, bf16[2304,1,128]{0,2,1:T(8,128)(2,1)S(1)}, u32[]{:S(2)}, u32[]{:S(2)}) collective-permute-start(bf16[2304,1,128]{0,2,1:T(8,128)(2,1)S(1)} %get-tuple-element.46), channel_id=1, source_target_pairs={{1,0},{3,2},{5,4},{7,6},{9,8},{11,10},{13,12},{15,14},{17,16},{19,... | collective-permute-start | bytes 1769480 | tf_op jit(solution)/shard_map/ppermute | solution.py:17
  (6 other events, 83.3 us)
Sparse Core Ops, SparseCore 0:
  10.9 90.3 all-gather.1
where the time goes:
time: 513 us; the launch traced here: 505 us
  waiting for transfers between devices  317 us (62%)
  matrix products  83 us (16%)
  starting transfers between devices  61.7 us (12%)
  other arithmetic  15.7 us (3%)
  between operations  14.4 us (3%)
  local copies, waits for them, and re-layouts  12.8 us (2%)
    ppermute x21, waiting for transfers between devices, hop(): return lax.ppermute(values, axis, pairs)  180 us
    all_gather x1, waiting for transfers between devices, on_device(): planes = lax.all_gather(distribution, 'vout', axis=0, tiled=True)  90.5 us
    dot_general x3, matrix products, on_device(): away = jnp.einsum(spec, block, theirs, preferred_element_type=jnp.float32)  42.1 us
    dot_general x3, matrix products, on_device(): near = jnp.einsum(spec, block, mine, preferred_element_type=jnp.float32)  40.9 us
    ppermute x21, starting transfers between devices, hop(): return lax.ppermute(values, axis, pairs)  37.8 us
    ppermute x6, waiting for transfers between devices, from_higher(): return lax.ppermute(values, axis, [(i + 1, i) for i in range(ends)])  28.7 us
    ppermute x6, waiting for transfers between devices, from_lower(): return lax.ppermute(values, axis, [(i, i + 1) for i in range(ends)])  18 us
    ppermute x6, starting transfers between devices, from_lower(): return lax.ppermute(values, axis, [(i, i + 1) for i in range(ends)])  12.6 us
  transfers between devices with their start and end apart: 34, of which 16 were waited for; matrix products, arithmetic and copies ran while one was open for 17% of the time, Pallas kernels for 0%

commit v1 on v0

v1 whole, which is shorter than its diff:
```python
import functools

import jax
import jax.numpy as jnp
from jax import lax
from jax.experimental import pallas as pl
from jax.experimental.pallas import tpu as pltpu
from jax.sharding import PartitionSpec as P

MESH = pl.DeviceIdType.MESH
CORES = 2
LANES = 128
BLOCK = 16


def rows_of(half):
    for rows in (576, 432, 288, 144, 96, 48, 16):
        if half % rows == 0:
            return rows
    return half


def kernel(
    size, dist, matrix, coef, fluid, out, lent,
    held, tile, sums, slots, weights, fluids,
    l_sem, cs_sem, cr_sem, xs_sem, xr_sem, hs_sem, hr_sem, gs_sem, gr_sem, ms_sem, mr_sem,
    fs_sem, fr_sem, t_sem, zs_sem, zr_sem, ol_sem, os_sem, or_sem,
):
    n, groups, planes, depth, half, rows, pieces = size
    total = n * CORES
    chunks = half // rows
    part = rows // pieces
    wide = 2 * LANES
    vin, x, y = lax.axis_index("vin"), lax.axis_index("vout"), lax.axis_index("cell")
    k, c = vin // CORES, lax.rem(vin, CORES)
    partner = {"vin": k * CORES + 1 - c}
    mirror = 2 * x >= groups
    staged = groups == 2 and n == 4 and planes == 4

    def remote(src, dst, send, recv, where):
        return pltpu.make_async_remote_copy(
            src_ref=src, dst_ref=dst, send_sem=send, recv_sem=recv, device_id=where, device_id_type=MESH
        )

    def other_group(j):
        return lax.rem(x + j, groups)

    everyone = [{"vin": lax.rem(vin + j, total)} for j in range(1, total)]
    for j in range(groups):
        if j:
            everyone.append({"vout": other_group(j)})
        everyone.append({"vout": other_group(j), "cell": 1 - y})
    barrier = pltpu.get_barrier_semaphore()
    for where in everyone:
        pl.semaphore_signal(barrier, inc=1, device_id=where, device_id_type=MESH)
    pl.semaphore_wait(barrier, len(everyone))

    def order(t):
        at = jnp.where(mirror, n - 1 - k, k)
        usual = jnp.where(t < 2, t, n + 1 - t)
        first = jnp.where(t == 0, 1, jnp.where(t == 1, n - 1, jnp.where(t == 2, 0, n + 1 - t)))
        g = jnp.where(at == 0, first, usual)
        return jnp.where(mirror, n - 1 - g, g)

    def item(s):
        j = s - chunks
        early, late = s < chunks, s >= (n - 1) * chunks
        t = jnp.where(early, 0, jnp.where(late, n - 1, 1 + lax.rem(j, n - 2)))
        i = jnp.where(early, s, jnp.where(late, s - (n - 1) * chunks, j // (n - 2)))
        return order(t), i

    mine = pl.ds(pl.multiple_of(c * depth, 16), depth)
    theirs = pl.ds(pl.multiple_of((1 - c) * depth, 16), depth)
    inner = pl.ds(pl.multiple_of((1 - y) * LANES, LANES), LANES)

    def halo_lanes(p):
        return pl.ds(pl.multiple_of(lax.rem(p, 2) * LANES, LANES), LANES)

    def local_plane(q):
        return pltpu.make_async_copy(dist.at[q], held.at[x * planes + q, mine], l_sem.at[q])

    def core_own(q):
        p = x * planes + q
        return remote(dist.at[q], held.at[p, mine], cs_sem.at[p], cr_sem.at[p], partner)

    def core_pass(p):
        return remote(held.at[p, mine], held.at[p, mine], cs_sem.at[p], cr_sem.at[p], partner)

    def core_got(p):
        return remote(held.at[p, theirs], held.at[p, theirs], cs_sem.at[p], cr_sem.at[p], partner)

    def main_send(to, q):
        p = x * planes + q
        return remote(dist.at[q], held.at[p, mine], xs_sem.at[to, q], xr_sem.at[p], {"vout": to})

    def main_got(p):
        return remote(held.at[p, mine], held.at[p, mine], xs_sem.at[0, 0], xr_sem.at[p], {"vout": other_group(1)})

    def halo_send(to, q):
        p = x * planes + q
        return remote(
            dist.at[q, :, inner], held.at[total + p // 2, mine, halo_lanes(p)], hs_sem.at[to, q], hr_sem.at[p],
            {"vout": to, "cell": 1 - y},
        )

    def halo_got(p):
        ref = held.at[total + p // 2, mine, halo_lanes(p)]
        return remote(ref, ref, hs_sem.at[0, 0], hr_sem.at[p], {"cell": 1 - y})

    def halo_pass(p):
        ref = held.at[total + p // 2, mine, halo_lanes(p)]
        return remote(ref, ref, gs_sem.at[p], gr_sem.at[p], partner)

    def halo_end(p):
        ref = held.at[total + p // 2, theirs, halo_lanes(p)]
        return remote(ref, ref, gs_sem.at[p], gr_sem.at[p], partner)

    def own_half(i):
        return pl.ds(pl.multiple_of(c * half + i * rows, 16), rows)

    def matrix_send(i):
        start = pl.multiple_of((1 - c) * half + i * rows, 16)
        return remote(
            matrix.at[pl.ds(start, rows)], lent.at[pl.ds(i * rows, rows)], ms_sem.at[i], mr_sem.at[i], partner
        )

    def flag_send(j):
        to = lax.rem(vin + j, total)
        return remote(fluid, fluids.at[vin], fs_sem.at[to], fr_sem.at[vin], {"vin": to})

    def flag_got(j):
        at = lax.rem(vin + j, total)
        return remote(fluid, fluids.at[at], fs_sem.at[at], fr_sem.at[at], {"vin": at})

    def load(s, which):
        i = item(s)[1]
        slot = lax.rem(s, 2)
        if which == 0:
            src, at = matrix.at[own_half(i)], c
        else:
            src, at = lent.at[pl.ds(pl.multiple_of(i * rows, 16), rows)], 1 - c
        return pltpu.make_async_copy(src, tile.at[slot, at], t_sem.at[slot, which])

    def coef_load():
        return pltpu.make_async_copy(
            coef.at[pl.ds(pl.multiple_of(c * half, 16), half)], weights, l_sem.at[planes]
        )

    first_pair = lax.rem(order(0), planes // 2)

    def halo_order(j):
        if not staged:
            return j
        pair = first_pair if j < 2 else 1 - first_pair
        return pair * 2 + j % 2

    def away(to, j):
        return jnp.where(x > to, j, planes - 1 - j)

    def from_group(src, j):
        return src * planes + jnp.where(src > x, j, planes - 1 - j)

    for q in range(planes):
        core_own(q).start()
        local_plane(q).start()
    for j in range(min(2, planes)):
        halo_send(x, halo_order(j)).start()
    for m in range(1, groups):
        to = other_group(m)
        main_send(to, away(to, 0)).start()
    matrix_send(0).start()
    load(0, 0).start()
    coef_load().start()
    for j in range(1, total):
        flag_send(j).start()
    for i in range(1, chunks):
        matrix_send(i).start()
    for j in range(2, planes):
        halo_send(x, halo_order(j)).start()
    for m in range(1, groups):
        to = other_group(m)
        for j in range(1, planes):
            main_send(to, away(to, j)).start()
        for j in list(range(2, planes)) + list(range(min(2, planes))):
            halo_send(to, away(to, j)).start()
    fluids[vin] = fluid[...]
    mr0 = matrix_send(0)
    mr0.wait_recv()
    load(0, 1).start()
    for j in range(1, total):
        flag_got(j).wait_recv()

    own = [x * planes + halo_order(j) for j in range(planes)]

    def pass_halo(ps):
        for p in ps:
            halo_got(p).wait_recv()
            halo_pass(p).start()

    def end_halo(ps):
        for p in ps:
            halo_end(p).wait_recv()

    def pass_main(ps):
        for p in ps:
            main_got(p).wait_recv()
            core_pass(p).start()

    def end_main(ps):
        for p in ps:
            core_got(p).wait_recv()

    near = [from_group(other_group(m), 0) for m in range(1, groups)]
    far = [from_group(other_group(m), j) for m in range(1, groups) for j in range(1, planes)]
    far_halo = [from_group(other_group(m), j) for m in range(1, groups) for j in range(2, planes)]
    near_halo = [from_group(other_group(m), j) for m in range(1, groups) for j in range(min(2, planes))]

    for q in range(planes):
        local_plane(q).wait()
    coef_load().wait()
    end_main([x * planes + q for q in range(planes)])
    pass_halo(own[:2])
    pass_main(near)
    end_halo(own[:2])
    end_main(near)

    def stage_two():
        pass_halo(own[2:])
        pass_main(far)
        pass_halo(far_halo)
        end_halo(own[2:])
        end_main(far)
        end_halo(far_halo)

    def stage_three():
        pass_halo(near_halo)
        end_halo(near_halo)

    if not staged:
        stage_two()
        stage_three()

    lane = lax.broadcasted_iota(jnp.int32, (BLOCK, LANES), 1)

    def message(g, m):
        up = g > k
        chip = jnp.clip(jnp.where(up, k + 1, k - 1), 0, n - 1)
        slot = jnp.where(up | (chip != g), g, n)
        at = pl.ds(pl.multiple_of(m * part, 16), part)
        return remote(
            slots.at[g, at], slots.at[slot, at], zs_sem.at[g, m], zr_sem.at[slot, m], {"vin": chip * CORES + c}
        )

    def arrival(slot, m):
        ref = slots.at[slot, pl.ds(pl.multiple_of(m * part, 16), part)]
        return remote(ref, ref, zs_sem.at[0, 0], zr_sem.at[slot, m], partner)

    def give(i):
        at = pl.ds(pl.multiple_of(i * rows, 16), rows)
        lanes = pl.ds(pl.multiple_of((1 - c) * wide, LANES), wide)
        return remote(slots.at[n + 1, at, lanes], out.at[own_half(i)], os_sem.at[i], or_sem.at[i], partner)

    def given(i):
        at = pl.ds(pl.multiple_of(i * rows, 16), rows)
        lanes = pl.ds(pl.multiple_of(c * wide, LANES), wide)
        dst = out.at[pl.ds(pl.multiple_of((1 - c) * half + i * rows, 16), rows)]
        return remote(slots.at[n + 1, at, lanes], dst, os_sem.at[i], or_sem.at[i], partner)

    def keep(i):
        at = pl.ds(pl.multiple_of(i * rows, 16), rows)
        lanes = pl.ds(pl.multiple_of(c * wide, LANES), wide)
        return pltpu.make_async_copy(slots.at[n + 1, at, lanes], out.at[own_half(i)], ol_sem.at[i])

    def step(s, carry):
        g, i = item(s)
        slot = lax.rem(s, 2)
        if staged:
            pl.when(s == chunks)(stage_two)
            pl.when(s == (n - 1) * chunks)(stage_three)
        load(s, 0).wait()
        load(s, 1).wait()

        @pl.when(s + 1 < n * chunks)
        def _():
            @pl.when(s + 1 < chunks)
            def _():
                nxt = jnp.minimum(s + 1, chunks - 1)
                remote(
                    lent.at[pl.ds(pl.multiple_of(nxt * rows, 16), rows)],
                    lent.at[pl.ds(pl.multiple_of(nxt * rows, 16), rows)],
                    ms_sem.at[nxt], mr_sem.at[nxt], partner,
                ).wait_recv()

            load(s + 1, 0).start()
            load(s + 1, 1).start()

        def product(j, carry):
            index = jnp.where(j == 4, total + g, jnp.clip(2 * g - 1 + j, 0, total - 1))
            outside = ((j == 0) & (g == 0)) | ((j == 3) & (g == n - 1))

            @pl.when(outside)
            def _():
                sums[j] = jnp.zeros((rows, wide), jnp.float32)

            @pl.when(jnp.logical_not(outside))
            def _():
                sums[j] = jnp.dot(
                    tile[slot, 0], held[index, pl.ds(0, depth)], preferred_element_type=jnp.float32
                ) + jnp.dot(tile[slot, 1], held[index, pl.ds(depth, depth)], preferred_element_type=jnp.float32)

            return carry

        lax.fori_loop(0, 5, product, 0)

        through = ((g > k) & (k > 0)) | ((g < k) & (k < n - 1))
        into = jnp.where(g == k, n + 1, g)

        def piece(m, carry):
            at = i * pieces + m
            pl.when(through)(lambda: arrival(g, at).wait_recv())

            def block(b, carry):
                r = pl.multiple_of(m * part + b * BLOCK, BLOCK)
                whole = pl.multiple_of(i * rows + m * part + b * BLOCK, BLOCK)
                here = pl.ds(r, BLOCK)
                w = weights[pl.ds(whole, BLOCK), :]
                wxl, wxh, wyl, wyh, wzl, wzh, ws = (w[:, e : e + 1] for e in range(7))
                for t in range(2):
                    for row in range(2):
                        lanes = slice(row * LANES, (row + 1) * LANES)
                        rest = slice((1 - row) * LANES, (2 - row) * LANES)
                        value = sums[1 + t, here, lanes]
                        along = sums[1 + t, here, rest]
                        halo = sums[4, here, t * LANES : (t + 1) * LANES]
                        xl = jnp.where(lane == 0, 0.0, pltpu.roll(value, 1, 1))
                        xh = jnp.where(lane == LANES - 1, 0.0, pltpu.roll(value, LANES - 1, 1))
                        if row == 0:
                            yl, yh = jnp.where(y == 1, halo, 0.0), along
                        else:
                            yl, yh = along, jnp.where(y == 0, halo, 0.0)
                        zl, zh = sums[t, here, lanes], sums[2 + t, here, lanes]
                        flow = wxl * xl + wxh * xh + wyl * yl + wyh * yh + wzl * zl + wzh * zh
                        free = fluids[2 * g + t, :, lanes]
                        moved = value - free * (ws * value - flow)
                        there = slice((2 * t + row) * LANES, (2 * t + row + 1) * LANES)
                        before = slots[into, pl.ds(whole, BLOCK), there].astype(jnp.float32)
                        moved = moved + jnp.where(through, before, 0.0)
                        slots[into, pl.ds(whole, BLOCK), there] = moved.astype(jnp.bfloat16)
                return carry

            lax.fori_loop(0, part // BLOCK, block, 0)
            pl.when(g != k)(lambda: message(g, at).start())
            return carry

        lax.fori_loop(0, pieces, piece, 0)

        @pl.when(s >= (n - 1) * chunks)
        def _():
            def settle(m, carry):
                at = i * pieces + m
                pl.when(k > 0)(lambda: arrival(k, at).wait_recv())
                pl.when(k < n - 1)(lambda: arrival(n, at).wait_recv())

                def block(b, carry):
                    here = pl.ds(pl.multiple_of(at * part + b * BLOCK, BLOCK), BLOCK)
                    low = slots[k, here, :].astype(jnp.float32)
                    high = slots[n, here, :].astype(jnp.float32)
                    value = slots[n + 1, here, :].astype(jnp.float32)
                    value = value + jnp.where(k > 0, low, 0.0) + jnp.where(k < n - 1, high, 0.0)
                    slots[n + 1, here, :] = value.astype(jnp.bfloat16)
                    return carry

                lax.fori_loop(0, part // BLOCK, block, 0)
                return carry

            lax.fori_loop(0, pieces, settle, 0)
            keep(i).start()
            give(i).start()

        return carry

    lax.fori_loop(0, n * chunks, step, 0)

    def finish(i, carry):
        keep(i).wait()
        give(i).wait_send()
        given(i).wait_recv()
        matrix_send(i).wait_send()
        return carry

    lax.fori_loop(0, chunks, finish, 0)

    def sent(g, carry):
        @pl.when(g != k)
        def _():
            def one(m, carry):
                message(g, m).wait_send()
                return carry

            lax.fori_loop(0, chunks * pieces, one, 0)

        return carry

    lax.fori_loop(0, n, sent, 0)
    for j in range(1, total):
        flag_send(j).wait_send()
    for q in range(planes):
        core_own(q).wait_send()
        halo_send(x, q).wait_send()
        halo_pass(x * planes + q).wait_send()
        for m in range(1, groups):
            to = other_group(m)
            main_send(to, q).wait_send()
            halo_send(to, q).wait_send()
            core_pass(to * planes + q).wait_send()
            halo_pass(to * planes + q).wait_send()


def on_device(chips, groups, distribution, collision, speeds, directions, cell_flags):
    planes, depth = distribution.shape[:2]
    velocities = collision.shape[0]
    half = velocities // CORES
    rows = rows_of(half)
    pieces = 2 if rows % 32 == 0 else 1
    total = chips * CORES
    wide = 2 * LANES
    chunks = half // rows
    dist = distribution.reshape(planes, depth, wide)
    lower = jnp.where(directions == 1, speeds, 0.0)
    upper = jnp.where(directions == 1, 0.0, speeds)
    coef = jnp.stack(
        [lower[0], upper[0], lower[1], upper[1], lower[2], upper[2], speeds[0] + speeds[1] + speeds[2], speeds[0]], axis=1
    )
    fluid = jnp.broadcast_to((1 - cell_flags).astype(jnp.float32).reshape(1, wide), (BLOCK, wide))
    any_space = pl.BlockSpec(memory_space=pl.ANY)
    dma = pltpu.SemaphoreType.DMA
    size = (chips, groups, planes, depth, half, rows, pieces)
    flops = 2 * half * 2 * depth * 5 * wide * chips
    out, _ = pl.pallas_call(
        functools.partial(kernel, size),
        out_shape=(
            jax.ShapeDtypeStruct((velocities, wide), jnp.bfloat16),
            jax.ShapeDtypeStruct((half, depth), jnp.bfloat16),
        ),
        in_specs=[any_space, any_space, any_space, pl.BlockSpec(memory_space=pltpu.VMEM)],
        out_specs=(any_space, any_space),
        scratch_shapes=[
            pltpu.VMEM((total + chips, CORES * depth, wide), jnp.bfloat16),
            pltpu.VMEM((2, CORES, rows, depth), jnp.bfloat16),
            pltpu.VMEM((5, rows, wide), jnp.float32),
            pltpu.VMEM((chips + 2, half, 2 * wide), jnp.bfloat16),
            pltpu.VMEM((half, 8), jnp.float32),
            pltpu.VMEM((total, BLOCK, wide), jnp.float32),
            dma((planes + 1,)),
            dma((total,)), dma((total,)),
            dma((groups, planes)), dma((total,)),
            dma((groups, planes)), dma((total,)),
            dma((total,)), dma((total,)),
            dma((chunks,)), dma((chunks,)),
            dma((total,)), dma((total,)),
            dma((2, 2)),
            dma((chips, chunks * pieces)), dma((chips + 1, chunks * pieces)),
            dma((chunks,)), dma((chunks,)), dma((chunks,)),
        ],
        compiler_params=pltpu.CompilerParams(
            collective_id=0, has_side_effects=True, vmem_limit_bytes=60 << 20
        ),
        cost_estimate=pl.CostEstimate(flops=flops, bytes_accessed=half * depth * 4 * chips, transcendentals=0),
    )(dist, collision, coef, fluid)
    return out.reshape(1, velocities, 2, LANES)


def solution(mesh):
    return jax.shard_map(
        functools.partial(on_device, mesh.shape["vin"] // CORES, mesh.shape["vout"]),
        mesh=mesh,
        in_specs=(
            P("vout", "vin", "cell", None),
            P("vout", "vin"),
            P(None, "vout"),
            P(None, "vout"),
            P("vin", "cell", None),
        ),
        out_specs=P("vin", "vout", "cell", None),
        check_vma=False,
    )
```

time: 513 us -> 403 us (0.79)
  Pallas kernels: 0 us -> 340 us
  waiting for transfers between devices: 317 us -> 0 us
  matrix products: 83 us -> 0 us
  starting transfers between devices: 61.7 us -> 0 us
  local copies, waits for them, and re-layouts: 12.8 us -> 50.9 us
  between operations: 14.4 us -> 0.02 us
  other arithmetic: 15.7 us -> 4.49 us
    pallas_call x0 -> x1, Pallas kernels: none -> 340 us  [on_device(): pl.pallas_call(functools.partial(kernel, size), out_shape=(jax.ShapeDtype...]
    ppermute x33 -> x0, waiting for transfers between devices: 227 us -> none  [the longest x21 180 us: hop(): return lax.ppermute(values, axis, pairs)]
    all_gather x1 -> x0, waiting for transfers between devices: 90.5 us -> none  [on_device(): planes = lax.all_gather(distribution, 'vout', axis=0, tiled=True)]
    dot_general x6 -> x0, matrix products: 83 us -> none  [the longest x3 42.1 us: on_device(): away = jnp.einsum(spec, block, theirs, preferred_element_type=jnp.float32)]
    ppermute x33 -> x0, starting transfers between devices: 61.7 us -> none  [the longest x21 37.8 us: hop(): return lax.ppermute(values, axis, pairs)]
    unnamed x9 -> x3, local copies, waits for them, and re-layouts: 4.26 us -> 31.2 us
    convert_element_type x15 -> x0, other arithmetic: 15.3 us -> none  [the longest x3 6.57 us: transport(): return (middle - fluid[None] * flux).astype(jnp.bfloat16)]
    reshape x0 -> x2, local copies, waits for them, and re-layouts: none -> 11.8 us  [the longest x1 7.83 us: on_device(): return out.reshape(1, velocities, 2, LANES)]
  transfers between devices with their start and end apart: 34 -> 0, of which waited for: 16 -> 0; matrix products, arithmetic and copies ran while one was open for 17% -> 0% of each run, Pallas kernels for 0% -> 0%
where the time goes in v1:
time: 403 us; the launch traced here: 395 us
  Pallas kernels  340 us (84%)
  local copies, waits for them, and re-layouts  50.9 us (13%)
  other arithmetic  4.49 us (1%)
    pallas_call x1, Pallas kernels, on_device(): pl.pallas_call(functools.partial(kernel, size), out_shape=(jax.ShapeDtype...  340 us
    unnamed x3, local copies, waits for them, and re-layouts  31.2 us

profile of v1, /device:TPU:8, one launch (start us, length us, event | category | flops | bytes accessed | tf_op | source)
XLA Modules:
  0.0 395.3 jit_solution(16481102572376425841)
XLA Ops:
  0.0 0.0 copy-start
  0.0 0.8 convert_bitcast_fusion
  0.8 0.6 broadcast_in_dim.15.fluid
  1.4 1.7 bitcast_add_fusion
  3.1 1.5 slice_bitcast_fusion.6
  4.7 1.0 broadcast_select_fusion
  5.7 0.9 broadcast_select_fusion.1
  6.6 0.8 slice_bitcast_fusion
  7.4 1.8 stack.4
  9.2 3.2 copy.19.coef
  12.4 0.0 copy-done
  12.4 3.9 reshape.35.dist
  16.4 31.2 %copy.18.matrix = bf16[6912,1728]{1,0:T(8,128)(2,1)} copy(bf16[6912,1728]{0,1:T(8,128)(2,1)} %param.6) | data formatting | bytes 47775744 | tf_op args[1]
  47.6 339.9 %shard_map.55 = (bf16[6912,256]{1,0:T(8,128)(2,1)}, bf16[3456,1728]{1,0:T(8,128)(2,1)}) custom-call(bf16[4,1728,256]{2,1,0:T(8,128)(2,1)} %reshape.35.dist, bf16[6912,1728]{1,0:T(8,128)(2,1)} %copy.18.matrix, f32[6912,8]{1,0:T(8,128)} %copy.19.coef, f32[16,256]{1,0:T(8,128)} %broadcast_in_dim.15.fluid), custom_call_target="tpu_custom_call" | custom-call | flops 122305904640 | bytes 95551488 | tf_op jit(solution)/shard_map/pallas_call | solution.py:439
  387.5 7.8 %reshape.36 = bf16[1,6912,2,128]{3,2,1,0:T(2,128)(2,1)} reshape(bf16[6912,256]{1,0:T(8,128)(2,1)} %get-tuple-element.6) | data formatting | bytes 7077888 | tf_op jit(solution)/shard_map/reshape | solution.py:470
Async XLA Ops:
  0.0 12.4 %copy-start = (bf16[4,1728,2,128]{3,2,1,0:T(2,128)(2,1)S(1)}, bf16[4,1728,2,128]{3,2,1,0:T(2,128)(2,1)}, u32[]{:S(2)}) copy-start(bf16[4,1728,2,128]{3,2,1,0:T(2,128)(2,1)} %param.5) | copy-start | bytes 10616836

commit v2 on v1

v2 whole, which is shorter than its diff:
```python
import functools

import jax
import jax.numpy as jnp
from jax import lax
from jax.experimental import pallas as pl
from jax.experimental.pallas import tpu as pltpu
from jax.sharding import PartitionSpec as P

MESH = pl.DeviceIdType.MESH
CORES = 2
LANES = 128
BLOCK = 16


def stripes(velocities):
    width = 2 * LANES if velocities % (2 * LANES) == 0 else LANES
    return width, pl.cdiv(velocities // width, CORES)


def kernel(
    size, dist, matrix, speeds, directions, fluid, out, lent,
    held, tile, sums, slots, flat, fluids,
    l_sem, cs_sem, cr_sem, xs_sem, xr_sem, hs_sem, hr_sem, gs_sem, gr_sem, ms_sem, mr_sem,
    fs_sem, fr_sem, t_sem, zs_sem, zr_sem, ol_sem, os_sem, or_sem,
):
    n, groups, planes, depth, width, most, least = size
    total = n * CORES
    strips = width // LANES
    wide = 2 * LANES
    vin, x, y = lax.axis_index("vin"), lax.axis_index("vout"), lax.axis_index("cell")
    k, c = vin // CORES, lax.rem(vin, CORES)
    partner = {"vin": k * CORES + 1 - c}
    chunks = jnp.where(c == 0, most, least)
    first_chunk, other_first = c * most, (1 - c) * most
    other_chunks = jnp.where(c == 0, least, most)
    mirror = 2 * x >= groups
    staged = groups == 2 and n == 4 and planes == 4

    def remote(src, dst, send, recv, where):
        return pltpu.make_async_remote_copy(
            src_ref=src, dst_ref=dst, send_sem=send, recv_sem=recv, device_id=where, device_id_type=MESH
        )

    def other_group(j):
        return lax.rem(x + j, groups)

    everyone = [{"vin": lax.rem(vin + j, total)} for j in range(1, total)]
    for j in range(groups):
        if j:
            everyone.append({"vout": other_group(j)})
        everyone.append({"vout": other_group(j), "cell": 1 - y})
    barrier = pltpu.get_barrier_semaphore()
    for where in everyone:
        pl.semaphore_signal(barrier, inc=1, device_id=where, device_id_type=MESH)
    pl.semaphore_wait(barrier, len(everyone))

    def order(t):
        at = jnp.where(mirror, n - 1 - k, k)
        usual = jnp.where(t < 2, t, n + 1 - t)
        first = jnp.where(t == 0, 1, jnp.where(t == 1, n - 1, jnp.where(t == 2, 0, n + 1 - t)))
        g = jnp.where(at == 0, first, usual)
        return jnp.where(mirror, n - 1 - g, g)

    def item(s):
        j = s - chunks
        early, late = s < chunks, s >= (n - 1) * chunks
        t = jnp.where(early, 0, jnp.where(late, n - 1, 1 + lax.rem(j, n - 2)))
        i = jnp.where(early, s, jnp.where(late, s - (n - 1) * chunks, j // (n - 2)))
        return order(t), i

    inner = pl.ds(pl.multiple_of((1 - y) * LANES, LANES), LANES)

    def main_of(p):
        return pl.ds(pl.multiple_of(p * wide, wide), wide)

    def halo_of(p):
        return pl.ds(pl.multiple_of(total * wide + p * LANES, LANES), LANES)

    def local_plane(q):
        return pltpu.make_async_copy(dist.at[q], held.at[c, main_of(x * planes + q)], l_sem.at[q])

    def core_own(q):
        p = x * planes + q
        return remote(dist.at[q], held.at[c, main_of(p)], cs_sem.at[p], cr_sem.at[p], partner)

    def core_pass(p):
        return remote(held.at[c, main_of(p)], held.at[c, main_of(p)], cs_sem.at[p], cr_sem.at[p], partner)

    def core_got(p):
        return remote(held.at[1 - c, main_of(p)], held.at[1 - c, main_of(p)], cs_sem.at[p], cr_sem.at[p], partner)

    def main_send(to, q):
        p = x * planes + q
        return remote(dist.at[q], held.at[c, main_of(p)], xs_sem.at[to, q], xr_sem.at[p], {"vout": to})

    def main_got(p):
        return remote(held.at[c, main_of(p)], held.at[c, main_of(p)], xs_sem.at[0, 0], xr_sem.at[p], {"vout": other_group(1)})

    def halo_send(to, q):
        p = x * planes + q
        return remote(
            dist.at[q, inner], held.at[c, halo_of(p)], hs_sem.at[to, q], hr_sem.at[p],
            {"vout": to, "cell": 1 - y},
        )

    def halo_got(p):
        ref = held.at[c, halo_of(p)]
        return remote(ref, ref, hs_sem.at[0, 0], hr_sem.at[p], {"cell": 1 - y})

    def halo_pass(p):
        ref = held.at[c, halo_of(p)]
        return remote(ref, ref, gs_sem.at[p], gr_sem.at[p], partner)

    def halo_end(p):
        ref = held.at[1 - c, halo_of(p)]
        return remote(ref, ref, gs_sem.at[p], gr_sem.at[p], partner)

    def lanes_of(chunk):
        return pl.ds(pl.multiple_of(chunk * width, LANES), width)

    def matrix_send(i):
        return remote(
            matrix.at[:, lanes_of(other_first + i)], lent.at[i], ms_sem.at[i], mr_sem.at[i], partner
        )

    def matrix_got(i):
        return remote(lent.at[i], lent.at[i], ms_sem.at[i], mr_sem.at[i], partner)

    def flag_send(j):
        to = lax.rem(vin + j, total)
        return remote(fluid, flat.at[vin], fs_sem.at[to], fr_sem.at[vin], {"vin": to})

    def flag_got(j):
        at = lax.rem(vin + j, total)
        return remote(fluid, flat.at[at], fs_sem.at[at], fr_sem.at[at], {"vin": at})

    def load(s, which):
        i = item(s)[1]
        slot = lax.rem(s, 2)
        if which == 0:
            src, at = matrix.at[:, lanes_of(first_chunk + i)], c
        else:
            src, at = lent.at[i], 1 - c
        return pltpu.make_async_copy(src, tile.at[slot, at], t_sem.at[slot, which])

    first_pair = lax.rem(order(0), planes // 2)

    def halo_order(j):
        if not staged:
            return j
        pair = first_pair if j < 2 else 1 - first_pair
        return pair * 2 + j % 2

    def away(to, j):
        return jnp.where(x > to, j, planes - 1 - j)

    def from_group(src, j):
        return src * planes + jnp.where(src > x, j, planes - 1 - j)

    for q in range(planes):
        core_own(q).start()
        local_plane(q).start()
    for j in range(min(2, planes)):
        halo_send(x, halo_order(j)).start()
    for m in range(1, groups):
        to = other_group(m)
        main_send(to, away(to, 0)).start()
    matrix_send(0).start()
    load(0, 0).start()
    for j in range(1, total):
        flag_send(j).start()

    def lend(i, carry):
        matrix_send(i).start()
        return carry

    lax.fori_loop(1, other_chunks, lend, 0)
    for j in range(2, planes):
        halo_send(x, halo_order(j)).start()
    for m in range(1, groups):
        to = other_group(m)
        for j in range(1, planes):
            main_send(to, away(to, j)).start()
        for j in list(range(2, planes)) + list(range(min(2, planes))):
            halo_send(to, away(to, j)).start()
    flat[vin] = fluid[...]
    matrix_got(0).wait_recv()
    load(0, 1).start()
    for j in range(1, total):
        flag_got(j).wait_recv()

    def spread(p, carry):
        for row in range(2):
            line = flat[p, 0:1, row * LANES : (row + 1) * LANES]
            fluids[p, row * LANES : (row + 1) * LANES] = jnp.broadcast_to(line, (LANES, LANES)).T
        return carry

    lax.fori_loop(0, total, spread, 0)

    own = [x * planes + halo_order(j) for j in range(planes)]

    def pass_halo(ps):
        for p in ps:
            halo_got(p).wait_recv()
            halo_pass(p).start()

    def end_halo(ps):
        for p in ps:
            halo_end(p).wait_recv()

    def pass_main(ps):
        for p in ps:
            main_got(p).wait_recv()
            core_pass(p).start()

    def end_main(ps):
        for p in ps:
            core_got(p).wait_recv()

    near = [from_group(other_group(m), 0) for m in range(1, groups)]
    far = [from_group(other_group(m), j) for m in range(1, groups) for j in range(1, planes)]
    far_halo = [from_group(other_group(m), j) for m in range(1, groups) for j in range(2, planes)]
    near_halo = [from_group(other_group(m), j) for m in range(1, groups) for j in range(min(2, planes))]

    for q in range(planes):
        local_plane(q).wait()
    end_main([x * planes + q for q in range(planes)])
    pass_halo(own[:2])
    pass_main(near)
    end_halo(own[:2])
    end_main(near)

    def stage_two():
        pass_halo(own[2:])
        pass_main(far)
        pass_halo(far_halo)
        end_halo(own[2:])
        end_main(far)
        end_halo(far_halo)

    def stage_three():
        pass_halo(near_halo)
        end_halo(near_halo)

    if not staged:
        stage_two()
        stage_three()

    near_row = lax.broadcasted_iota(jnp.int32, (BLOCK, LANES), 0)

    def message(g, i):
        up = g > k
        chip = jnp.clip(jnp.where(up, k + 1, k - 1), 0, n - 1)
        slot = jnp.where(up | (chip != g), g, n)
        return remote(
            slots.at[g, i], slots.at[slot, i], zs_sem.at[g, i], zr_sem.at[slot, i], {"vin": chip * CORES + c}
        )

    def arrival(slot, i):
        ref = slots.at[slot, i]
        return remote(ref, ref, zs_sem.at[0, 0], zr_sem.at[slot, i], partner)

    def place(chunk):
        return pl.ds(chunk * strips, strips)

    def plane_of(i, at):
        return slots.at[n + 1, i, :, pl.ds(pl.multiple_of(at * wide, wide), wide)]

    def give(i):
        return remote(
            plane_of(i, 1 - c), out.at[place(first_chunk + i)], os_sem.at[i], or_sem.at[first_chunk + i], partner
        )

    def given(i):
        dst = out.at[place(other_first + i)]
        return remote(dst, dst, os_sem.at[i], or_sem.at[other_first + i], partner)

    def keep(i):
        return pltpu.make_async_copy(plane_of(i, c), out.at[place(first_chunk + i)], ol_sem.at[i])

    def step(s, carry):
        g, i = item(s)
        slot = lax.rem(s, 2)
        if staged:
            pl.when(s == chunks)(stage_two)
            pl.when(s == (n - 1) * chunks)(stage_three)
        load(s, 0).wait()
        load(s, 1).wait()

        @pl.when(s + 1 < n * chunks)
        def _():
            @pl.when(s + 1 < chunks)
            def _():
                matrix_got(s + 1).wait_recv()

            load(s + 1, 0).start()
            load(s + 1, 1).start()

        def product(start, count, to):
            at = pl.ds(pl.multiple_of(start, wide), count)
            value = jnp.dot(held[0, at], tile[slot, 0], preferred_element_type=jnp.float32)
            value = value + jnp.dot(held[1, at], tile[slot, 1], preferred_element_type=jnp.float32)
            for q in range(strips):
                sums[q, to : to + count] = value[:, q * LANES : (q + 1) * LANES]

        @pl.when((g > 0) & (g < n - 1))
        def _():
            product((2 * g - 1) * wide, 4 * wide, 0)

        @pl.when(g == 0)
        def _():
            product(0, 3 * wide, wide)
            for q in range(strips):
                sums[q, 0:wide] = jnp.zeros((wide, LANES), jnp.float32)

        @pl.when(g == n - 1)
        def _():
            product((total - 3) * wide, 3 * wide, 0)
            for q in range(strips):
                sums[q, 3 * wide : 4 * wide] = jnp.zeros((wide, LANES), jnp.float32)

        product((total + g) * wide, wide, 4 * wide)

        through = ((g > k) & (k > 0)) | ((g < k) & (k < n - 1))
        into = jnp.where(g == k, n + 1, g)
        pl.when(through)(lambda: arrival(g, i).wait_recv())

        def move(q, carry):
            here = pl.ds(pl.multiple_of((first_chunk + i) * width + q * LANES, LANES), LANES)
            low, high = [], []
            for e in range(3):
                speed, ahead = speeds[e : e + 1, here], directions[e : e + 1, here] == 1
                low.append(jnp.broadcast_to(jnp.where(ahead, speed, 0.0), (BLOCK, LANES)))
                high.append(jnp.broadcast_to(jnp.where(ahead, 0.0, speed), (BLOCK, LANES)))
            whole = sum(low) + sum(high)
            outer_low = jnp.where(y == 1, low[1], 0.0)
            outer_high = jnp.where(y == 0, high[1], 0.0)
            for t in range(2):
                for row in range(2):
                    for b in range(LANES // BLOCK):
                        shift = b * BLOCK
                        base = (1 + t) * wide + row * LANES + shift
                        value = sums[q, base : base + BLOCK]
                        before = sums[q, base - 1 : base - 1 + BLOCK]
                        after = sums[q, base + 1 : base + 1 + BLOCK]
                        if b == 0:
                            before = jnp.where(near_row == 0, 0.0, before)
                        if shift + BLOCK == LANES:
                            after = jnp.where(near_row == BLOCK - 1, 0.0, after)
                        side = (1 + t) * wide + (1 - row) * LANES + shift
                        along = sums[q, side : side + BLOCK]
                        edge = 4 * wide + t * LANES + shift
                        halo = sums[q, edge : edge + BLOCK]
                        flow = low[0] * before + high[0] * after
                        if row == 0:
                            flow = flow + outer_low * halo + high[1] * along
                        else:
                            flow = flow + low[1] * along + outer_high * halo
                        flow = flow + low[2] * sums[q, base - wide : base - wide + BLOCK]
                        flow = flow + high[2] * sums[q, base + wide : base + wide + BLOCK]
                        free = fluids[2 * g + t, row * LANES + shift : row * LANES + shift + BLOCK]
                        moved = value - free * (whole * value - flow)
                        there = slice(base - wide, base - wide + BLOCK)
                        prior = slots[into, i, q, there].astype(jnp.float32)
                        moved = moved + jnp.where(through, prior, 0.0)
                        slots[into, i, q, there] = moved.astype(jnp.bfloat16)
            return carry

        lax.fori_loop(0, strips, move, 0)
        pl.when(g != k)(lambda: message(g, i).start())

        @pl.when(s >= (n - 1) * chunks)
        def _():
            pl.when(k > 0)(lambda: arrival(k, i).wait_recv())
            pl.when(k < n - 1)(lambda: arrival(n, i).wait_recv())

            def settle(b, carry):
                here = pl.ds(pl.multiple_of(b * 2 * BLOCK, 2 * BLOCK), 2 * BLOCK)
                for q in range(strips):
                    low = slots[k, i, q, here].astype(jnp.float32)
                    high = slots[n, i, q, here].astype(jnp.float32)
                    value = slots[n + 1, i, q, here].astype(jnp.float32)
                    value = value + jnp.where(k > 0, low, 0.0) + jnp.where(k < n - 1, high, 0.0)
                    slots[n + 1, i, q, here] = value.astype(jnp.bfloat16)
                return carry

            lax.fori_loop(0, wide // BLOCK, settle, 0)
            keep(i).start()
            give(i).start()

        return carry

    lax.fori_loop(0, n * chunks, step, 0)

    def finish(i, carry):
        keep(i).wait()
        give(i).wait_send()
        return carry

    lax.fori_loop(0, chunks, finish, 0)

    def returned(i, carry):
        given(i).wait_recv()
        matrix_send(i).wait_send()
        return carry

    lax.fori_loop(0, other_chunks, returned, 0)

    def sent(g, carry):
        @pl.when(g != k)
        def _():
            def one(m, carry):
                message(g, m).wait_send()
                return carry

            lax.fori_loop(0, chunks, one, 0)

        return carry

    lax.fori_loop(0, n, sent, 0)
    for j in range(1, total):
        flag_send(j).wait_send()
    for q in range(planes):
        core_own(q).wait_send()
        halo_send(x, q).wait_send()
        halo_pass(x * planes + q).wait_send()
        for m in range(1, groups):
            to = other_group(m)
            main_send(to, q).wait_send()
            halo_send(to, q).wait_send()
            core_pass(to * planes + q).wait_send()
            halo_pass(to * planes + q).wait_send()


def on_device(chips, groups, distribution, collision, speeds, directions, cell_flags):
    planes, depth = distribution.shape[:2]
    matrix = collision.T
    extra = -matrix.shape[1] % LANES
    if extra:
        matrix, speeds, directions = (jnp.pad(v, ((0, 0), (0, extra))) for v in (matrix, speeds, directions))
    velocities = matrix.shape[1]
    width, most = stripes(velocities)
    total = chips * CORES
    wide = 2 * LANES
    dist = distribution.transpose(0, 2, 3, 1).reshape(planes, wide, depth)
    fluid = jnp.broadcast_to((1 - cell_flags).astype(jnp.float32).reshape(1, wide), (8, wide))
    any_space = pl.BlockSpec(memory_space=pl.ANY)
    vmem = pl.BlockSpec(memory_space=pltpu.VMEM)
    dma = pltpu.SemaphoreType.DMA
    size = (chips, groups, planes, depth, width, most, velocities // width - most)
    flops = 2 * velocities * depth * 5 * wide * chips
    out, _ = pl.pallas_call(
        functools.partial(kernel, size),
        out_shape=(
            jax.ShapeDtypeStruct((velocities // LANES, wide, LANES), jnp.bfloat16),
            jax.ShapeDtypeStruct((most, depth, width), jnp.bfloat16),
        ),
        in_specs=[any_space, any_space, vmem, vmem, vmem],
        out_specs=(any_space, any_space),
        scratch_shapes=[
            pltpu.VMEM((CORES, (total + chips) * wide, depth), jnp.bfloat16),
            pltpu.VMEM((2, CORES, depth, width), jnp.bfloat16),
            pltpu.VMEM((width // LANES, 5 * wide, LANES), jnp.float32),
            pltpu.VMEM((chips + 2, most, width // LANES, 2 * wide, LANES), jnp.bfloat16),
            pltpu.VMEM((total, 8, wide), jnp.float32),
            pltpu.VMEM((total, wide, LANES), jnp.float32),
            dma((planes,)),
            dma((total,)), dma((total,)),
            dma((groups, planes)), dma((total,)),
            dma((groups, planes)), dma((total,)),
            dma((total,)), dma((total,)),
            dma((most,)), dma((most,)),
            dma((total,)), dma((total,)),
            dma((2, 2)),
            dma((chips, most)), dma((chips + 1, most)),
            dma((most,)), dma((most,)), dma((CORES * most,)),
        ],
        compiler_params=pltpu.CompilerParams(
            collective_id=0, has_side_effects=True, vmem_limit_bytes=60 << 20
        ),
        cost_estimate=pl.CostEstimate(flops=flops, bytes_accessed=velocities * depth * 2 * chips, transcendentals=0),
    )(dist, matrix, speeds, directions, fluid)
    out = out.reshape(velocities // LANES, 2, LANES, LANES).transpose(0, 3, 1, 2)
    return out.reshape(1, velocities, 2, LANES)[:, : velocities - extra]


def solution(mesh):
    return jax.shard_map(
        functools.partial(on_device, mesh.shape["vin"] // CORES, mesh.shape["vout"]),
        mesh=mesh,
        in_specs=(
            P("vout", "vin", "cell", None),
            P("vout", "vin"),
            P(None, "vout"),
            P(None, "vout"),
            P("vin", "cell", None),
        ),
        out_specs=P("vin", "vout", "cell", None),
        check_vma=False,
    )
```

time: 403 us -> 311 us (0.77); the launches traced: 395 us -> 307 us
  Pallas kernels: 340 us -> 286 us
  local copies, waits for them, and re-layouts: 50.9 us -> 20.3 us
    pallas_call x1, Pallas kernels: 340 us -> 286 us  [on_device(): pl.pallas_call(functools.partial(kernel, size), out_shape=(jax.ShapeDtype...]
    unnamed x3 -> x0, local copies, waits for them, and re-layouts: 31.2 us -> none
    transpose x0 -> x2, local copies, waits for them, and re-layouts: none -> 19.7 us  [the longest x1 9.88 us: on_device(): dist = distribution.transpose(0, 2, 3, 1).reshape(planes, wide, depth)]
    reshape x2 -> x0, local copies, waits for them, and re-layouts: 11.8 us -> none  [the longest x1 7.83 us: on_device(): return out.reshape(1, velocities, 2, LANES)]
    another operation x3 -> x0, local copies, waits for them, and re-layouts: 5.83 us -> none  [on_device(): jnp.stack([lower[0], upper[0], lower[1], upper[1], lower[2], upper[2], sp...]
where the time goes in v2:
time: 311 us; the launch traced here: 307 us
  Pallas kernels  286 us (92%)
  local copies, waits for them, and re-layouts  20.3 us (7%)
    pallas_call x1, Pallas kernels, on_device(): pl.pallas_call(functools.partial(kernel, size), out_shape=(jax.ShapeDtype...  286 us
    transpose x1, local copies, waits for them, and re-layouts, on_device(): dist = distribution.transpose(0, 2, 3, 1).reshape(planes, wide, depth)  9.88 us
    transpose x1, local copies, waits for them, and re-layouts, on_device(): out.reshape(velocities // LANES, 2, LANES, LANES).transpose(0, 3, 1, 2)  9.81 us

profile of v2, /device:TPU:8, one launch (start us, length us, event | category | flops | bytes accessed | tf_op | source)
XLA Modules:
  0.0 307.4 jit_solution(12725620534834484269)
XLA Ops:
  0.0 0.7 convert_bitcast_fusion
  0.7 0.6 broadcast_in_dim.8.fluid
  1.3 9.9 %copy.6 = bf16[4,2,128,1728]{3,2,1,0:T(8,128)(2,1)} copy(bf16[4,2,128,1728]{2,1,3,0:T(2,128)(2,1)} %bitcast.10) | data formatting | bytes 7077888 | tf_op jit(solution)/shard_map/transpose | solution.py:446
  11.2 286.4 %shard_map.55 = (bf16[54,256,128]{2,1,0:T(8,128)(2,1)}, bf16[14,1728,256]{2,1,0:T(8,128)(2,1)}) custom-call(bf16[4,256,1728]{2,1,0:T(8,128)(2,1)} %bitcast.9, bf16[1728,6912]{1,0:T(8,128)(2,1)} %bitcast.12, f32[3,6912]{1,0:T(4,128)} %speeds.1, s32[3,6912]{1,0:T(4,128)} %directions.1, f32[8,256]{1,0:T(8,128)} %broadcast_in_dim.8.fluid), custom_call_target="tpu_custom_call" | custom-call | flops 122305904640 | bytes 95551488 | tf_op jit(solution)/shard_map/pallas_call | solution.py:453
  297.6 9.8 %copy.7 = bf16[54,128,2,128]{3,2,1,0:T(2,128)(2,1)} copy(bf16[54,128,2,128]{1,3,2,0:T(8,128)(2,1)} %bitcast.11) | data formatting | bytes 7077888 | tf_op jit(solution)/shard_map/transpose | solution.py:484

commit v3 on v2

--- a/solution.py
+++ b/solution.py
@@ -11,6 +11,7 @@
 CORES = 2
 LANES = 128
 BLOCK = 16
+KEPT = 2
 
 
 def stripes(velocities):
@@ -20,7 +21,7 @@
 
 def kernel(
     size, dist, matrix, speeds, directions, fluid, out, lent,
-    held, tile, sums, slots, flat, fluids,
+    held, tile, sums, slots, flat, fluids, raw, spaced,
     l_sem, cs_sem, cr_sem, xs_sem, xr_sem, hs_sem, hr_sem, gs_sem, gr_sem, ms_sem, mr_sem,
     fs_sem, fr_sem, t_sem, zs_sem, zr_sem, ol_sem, os_sem, or_sem,
 ):
@@ -53,23 +54,43 @@
     barrier = pltpu.get_barrier_semaphore()
     for where in everyone:
         pl.semaphore_signal(barrier, inc=1, device_id=where, device_id_type=MESH)
-    pl.semaphore_wait(barrier, len(everyone))
-
-    def order(t):
-        at = jnp.where(mirror, n - 1 - k, k)
-        usual = jnp.where(t < 2, t, n + 1 - t)
-        first = jnp.where(t == 0, 1, jnp.where(t == 1, n - 1, jnp.where(t == 2, 0, n + 1 - t)))
-        g = jnp.where(at == 0, first, usual)
+
+    at = jnp.where(mirror, n - 1 - k, k)
+    final_chip = at == n - 1
+
+    def turned(g):
         return jnp.where(mirror, n - 1 - g, g)
 
+    first_group = turned(jnp.where(at == 0, 1, 0)) if staged else 0
+    steps = (n + 1) * chunks if staged else n * chunks
+    last = steps - chunks
+
     def item(s):
-        j = s - chunks
-        early, late = s < chunks, s >= (n - 1) * chunks
-        t = jnp.where(early, 0, jnp.where(late, n - 1, 1 + lax.rem(j, n - 2)))
-        i = jnp.where(early, s, jnp.where(late, s - (n - 1) * chunks, j // (n - 2)))
-        return order(t), i
-
-    inner = pl.ds(pl.multiple_of((1 - y) * LANES, LANES), LANES)
+        if not staged:
+            return s // chunks, lax.rem(s, chunks)
+        j = s - 2 * chunks
+        third, rest = j // 3, lax.rem(j, 3)
+        sent = 2 * third + rest
+        length = jnp.where(at == 2, chunks, chunks - KEPT)
+        one, two = sent < length, sent < length + chunks
+        g = jnp.where(rest == 2, at, jnp.where(one | jnp.logical_not(two), jnp.where(at == 2, 1, 2), 3))
+        i = jnp.where(rest == 2, third, jnp.where(one, sent, jnp.where(two, sent - length, sent - chunks)))
+        g = jnp.where(final_chip, 1 + j // chunks, g)
+        i = jnp.where(final_chip, lax.rem(s, chunks), i)
+        early = j < 0
+        return jnp.where(early, first_group, turned(g)), jnp.where(early, lax.rem(s, chunks), i)
+
+    inner, outer = 1 - y, y
+
+    def inner_of(p):
+        return pl.ds(pl.multiple_of(p * wide + inner * LANES, LANES), LANES)
+
+    diagonal = lax.broadcasted_iota(jnp.int32, (LANES, LANES), 0) == lax.broadcasted_iota(jnp.int32, (LANES, LANES), 1)
+    unit = jnp.where(diagonal, 1.0, 0.0).astype(jnp.bfloat16)
+
+    def flipped(values):
+        exact = lax.dot_general(unit, values, (((1,), (1,)), ((), ())), preferred_element_type=jnp.float32)
+        return exact.astype(jnp.bfloat16)
 
     def main_of(p):
         return pl.ds(pl.multiple_of(p * wide, wide), wide)
@@ -77,12 +98,18 @@
     def halo_of(p):
         return pl.ds(pl.multiple_of(total * wide + p * LANES, LANES), LANES)
 
-    def local_plane(q):
-        return pltpu.make_async_copy(dist.at[q], held.at[c, main_of(x * planes + q)], l_sem.at[q])
+    def fetch(q):
+        return pltpu.make_async_copy(dist.at[q], raw.at[q % 2], l_sem.at[q])
+
+    def turn(q):
+        spaced[...] = raw[q % 2].astype(jnp.float32)
+        for row in range(2):
+            values = spaced[pl.ds(row, depth, stride=2), :].astype(jnp.bfloat16)
+            at = pl.ds(pl.multiple_of((x * planes + q) * wide + row * LANES, LANES), LANES)
+            held[c, at] = flipped(values)
 
     def core_own(q):
-        p = x * planes + q
-        return remote(dist.at[q], held.at[c, main_of(p)], cs_sem.at[p], cr_sem.at[p], partner)
+        return core_pass(x * planes + q)
 
     def core_pass(p):
         return remote(held.at[c, main_of(p)], held.at[c, main_of(p)], cs_sem.at[p], cr_sem.at[p], partner)
@@ -92,7 +119,7 @@
 
     def main_send(to, q):
         p = x * planes + q
-        return remote(dist.at[q], held.at[c, main_of(p)], xs_sem.at[to, q], xr_sem.at[p], {"vout": to})
+        return remote(held.at[c, main_of(p)], held.at[c, main_of(p)], xs_sem.at[to, q], xr_sem.at[p], {"vout": to})
 
     def main_got(p):
         return remote(held.at[c, main_of(p)], held.at[c, main_of(p)], xs_sem.at[0, 0], xr_sem.at[p], {"vout": other_group(1)})
@@ -100,7 +127,7 @@
     def halo_send(to, q):
         p = x * planes + q
         return remote(
-            dist.at[q, inner], held.at[c, halo_of(p)], hs_sem.at[to, q], hr_sem.at[p],
+            held.at[c, inner_of(p)], held.at[c, halo_of(p)], hs_sem.at[to, q], hr_sem.at[p],
             {"vout": to, "cell": 1 - y},
         )
 
@@ -144,7 +171,7 @@
             src, at = lent.at[i], 1 - c
         return pltpu.make_async_copy(src, tile.at[slot, at], t_sem.at[slot, which])
 
-    first_pair = lax.rem(order(0), planes // 2)
+    first_pair = lax.rem(first_group, planes // 2)
 
     def halo_order(j):
         if not staged:
@@ -158,16 +185,23 @@
     def from_group(src, j):
         return src * planes + jnp.where(src > x, j, planes - 1 - j)
 
+    load(0, 0).start()
+    for q in range(min(2, planes)):
+        fetch(q).start()
     for q in range(planes):
+        fetch(q).wait()
+        turn(q)
+        if q + 2 < planes:
+            fetch(q + 2).start()
+        if q == 0:
+            pl.semaphore_wait(barrier, len(everyone))
+            matrix_send(0).start()
         core_own(q).start()
-        local_plane(q).start()
     for j in range(min(2, planes)):
         halo_send(x, halo_order(j)).start()
     for m in range(1, groups):
         to = other_group(m)
         main_send(to, away(to, 0)).start()
-    matrix_send(0).start()
-    load(0, 0).start()
     for j in range(1, total):
         flag_send(j).start()
 
@@ -180,11 +214,17 @@
         halo_send(x, halo_order(j)).start()
     for m in range(1, groups):
         to = other_group(m)
-        for j in range(1, planes):
+        for j in range(1, min(3, planes)):
             main_send(to, away(to, j)).start()
-        for j in list(range(2, planes)) + list(range(min(2, planes))):
+        for j in range(min(2, planes)):
+            halo_send(to, away(to, j)).start()
+        for j in range(3, planes):
+            main_send(to, away(to, j)).start()
+        for j in range(2, planes):
             halo_send(to, away(to, j)).start()
     flat[vin] = fluid[...]
+    for q in range(strips):
+        sums[q, 4 * wide : 5 * wide] = jnp.zeros((wide, LANES), jnp.float32)
     matrix_got(0).wait_recv()
     load(0, 1).start()
     for j in range(1, total):
@@ -218,48 +258,58 @@
         for p in ps:
             core_got(p).wait_recv()
 
-    near = [from_group(other_group(m), 0) for m in range(1, groups)]
-    far = [from_group(other_group(m), j) for m in range(1, groups) for j in range(1, planes)]
-    far_halo = [from_group(other_group(m), j) for m in range(1, groups) for j in range(2, planes)]
-    near_halo = [from_group(other_group(m), j) for m in range(1, groups) for j in range(min(2, planes))]
-
-    for q in range(planes):
-        local_plane(q).wait()
+    def others(low, high):
+        return [from_group(other_group(m), j) for m in range(1, groups) for j in range(low, min(high, planes))]
+
+    near, middle, far, near_halo, far_halo = others(0, 1), others(1, 3), others(3, 99), others(0, 2), others(2, 99)
     end_main([x * planes + q for q in range(planes)])
-    pass_halo(own[:2])
-    pass_main(near)
-    end_halo(own[:2])
-    end_main(near)
-
-    def stage_two():
-        pass_halo(own[2:])
-        pass_main(far)
-        pass_halo(far_halo)
-        end_halo(own[2:])
-        end_main(far)
-        end_halo(far_halo)
-
-    def stage_three():
-        pass_halo(near_halo)
-        end_halo(near_halo)
+
+    def at_step(s):
+        def when(step, *calls):
+            @pl.when(s == step)
+            def _():
+                for call, ps in calls:
+                    call(ps)
+
+        when(chunks - 4, (pass_halo, own[:2]), (pass_main, near))
+        when(chunks, (end_halo, own[:2]), (end_main, near))
+        when(2 * chunks - 3, (pass_halo, own[2:]), (pass_main, middle))
+        when(2 * chunks, (end_halo, own[2:]))
+        when(2 * chunks - 1, (pass_halo, near_halo))
+        when(jnp.where(final_chip, 3 * chunks, 2 * chunks), (end_main, middle), (end_halo, near_halo))
+        when(2 * chunks + 12, (pass_main, far), (pass_halo, far_halo))
+        when(2 * chunks + 15, (end_main, far), (end_halo, far_halo))
 
     if not staged:
-        stage_two()
-        stage_three()
+        pass_halo(own)
+        pass_main(near + middle + far)
+        pass_halo(near_halo + far_halo)
+        end_halo(own)
+        end_main(near + middle + far)
+        end_halo(near_halo + far_halo)
 
     near_row = lax.broadcasted_iota(jnp.int32, (BLOCK, LANES), 0)
 
-    def message(g, i):
+    parts = (pl.ds(0, LANES), pl.ds(LANES, 3 * LANES))
+
+    def message(g, i, part):
         up = g > k
         chip = jnp.clip(jnp.where(up, k + 1, k - 1), 0, n - 1)
         slot = jnp.where(up | (chip != g), g, n)
+        rows = parts[part]
         return remote(
-            slots.at[g, i], slots.at[slot, i], zs_sem.at[g, i], zr_sem.at[slot, i], {"vin": chip * CORES + c}
+            slots.at[g, i, :, rows], slots.at[slot, i, :, rows], zs_sem.at[part, g, i], zr_sem.at[part, slot, i],
+            {"vin": chip * CORES + c},
         )
 
-    def arrival(slot, i):
-        ref = slots.at[slot, i]
-        return remote(ref, ref, zs_sem.at[0, 0], zr_sem.at[slot, i], partner)
+    def arrival(slot, i, part):
+        ref = slots.at[slot, i, :, parts[part]]
+        return remote(ref, ref, zs_sem.at[0, 0, 0], zr_sem.at[part, slot, i], partner)
+
+    first_plane = jnp.where(mirror, 1, 0)
+
+    def spot(t, row):
+        return jnp.where(first_plane == t, 0, 2) + jnp.where(outer == row, 0, 1)
 
     def place(chunk):
         return pl.ds(chunk * strips, strips)
@@ -283,12 +333,11 @@
         g, i = item(s)
         slot = lax.rem(s, 2)
         if staged:
-            pl.when(s == chunks)(stage_two)
-            pl.when(s == (n - 1) * chunks)(stage_three)
+            at_step(s)
         load(s, 0).wait()
         load(s, 1).wait()
 
-        @pl.when(s + 1 < n * chunks)
+        @pl.when(s + 1 < steps)
         def _():
             @pl.when(s + 1 < chunks)
             def _():
@@ -304,27 +353,60 @@
             for q in range(strips):
                 sums[q, to : to + count] = value[:, q * LANES : (q + 1) * LANES]
 
-        @pl.when((g > 0) & (g < n - 1))
+        def clear(at):
+            for q in range(strips):
+                sums[q, at : at + wide] = jnp.zeros((wide, LANES), jnp.float32)
+
+        full = s >= chunks if staged else s >= 0
+
+        @pl.when(full)
         def _():
-            product((2 * g - 1) * wide, 4 * wide, 0)
-
-        @pl.when(g == 0)
-        def _():
-            product(0, 3 * wide, wide)
-            for q in range(strips):
-                sums[q, 0:wide] = jnp.zeros((wide, LANES), jnp.float32)
-
-        @pl.when(g == n - 1)
-        def _():
-            product((total - 3) * wide, 3 * wide, 0)
-            for q in range(strips):
-                sums[q, 3 * wide : 4 * wide] = jnp.zeros((wide, LANES), jnp.float32)
-
-        product((total + g) * wide, wide, 4 * wide)
+            @pl.when((g > 0) & (g < n - 1))
+            def _():
+                product((2 * g - 1) * wide, 4 * wide, 0)
+
+            @pl.when(g == 0)
+            def _():
+                product(0, 3 * wide, wide)
+                clear(0)
+
+            @pl.when(g == n - 1)
+            def _():
+                product((total - 3) * wide, 3 * wide, 0)
+                clear(3 * wide)
+
+            product((total + g) * wide, wide, 4 * wide)
+
+        if staged:
+
+            @pl.when(jnp.logical_not(full))
+            def _():
+                @pl.when(jnp.logical_not(mirror) & (g > 0))
+                def _():
+                    product((2 * g - 1) * wide, 3 * wide, 0)
+
+                @pl.when(jnp.logical_not(mirror) & (g == 0))
+                def _():
+                    product(0, 2 * wide, wide)
+                    clear(0)
+
+                @pl.when(mirror & (g < n - 1))
+                def _():
+                    product(2 * g * wide, 3 * wide, wide)
+
+                @pl.when(mirror & (g == n - 1))
+                def _():
+                    product(2 * g * wide, 2 * wide, wide)
+                    clear(3 * wide)
 
         through = ((g > k) & (k > 0)) | ((g < k) & (k < n - 1))
         into = jnp.where(g == k, n + 1, g)
-        pl.when(through)(lambda: arrival(g, i).wait_recv())
+        if staged:
+            does = (s < chunks) | (s >= 2 * chunks), s >= chunks
+        else:
+            does = s >= 0, s >= 0
+        for part in range(2):
+            pl.when(through & does[part])(lambda: arrival(g, i, part).wait_recv())
 
         def move(q, carry):
             here = pl.ds(pl.multiple_of((first_chunk + i) * width + q * LANES, LANES), LANES)
@@ -336,8 +418,11 @@
             whole = sum(low) + sum(high)
             outer_low = jnp.where(y == 1, low[1], 0.0)
             outer_high = jnp.where(y == 0, high[1], 0.0)
-            for t in range(2):
-                for row in range(2):
+            def quarter(t, row):
+                at = spot(t, row)
+
+                @pl.when(((at == 0) & does[0]) | ((at > 0) & does[1]))
+                def _():
                     for b in range(LANES // BLOCK):
                         shift = b * BLOCK
                         base = (1 + t) * wide + row * LANES + shift
@@ -361,37 +446,51 @@
                         flow = flow + high[2] * sums[q, base + wide : base + wide + BLOCK]
                         free = fluids[2 * g + t, row * LANES + shift : row * LANES + shift + BLOCK]
                         moved = value - free * (whole * value - flow)
-                        there = slice(base - wide, base - wide + BLOCK)
+                        there = pl.ds(pl.multiple_of(at * LANES + shift, BLOCK), BLOCK)
                         prior = slots[into, i, q, there].astype(jnp.float32)
                         moved = moved + jnp.where(through, prior, 0.0)
                         slots[into, i, q, there] = moved.astype(jnp.bfloat16)
+
+            for t in range(2):
+                for row in range(2):
+                    quarter(t, row)
             return carry
 
         lax.fori_loop(0, strips, move, 0)
-        pl.when(g != k)(lambda: message(g, i).start())
-
-        @pl.when(s >= (n - 1) * chunks)
+        for part in range(2):
+            pl.when((g != k) & does[part])(lambda: message(g, i, part).start())
+
+        f = s - last
+
+        @pl.when((f >= 0) & (f < chunks))
         def _():
-            pl.when(k > 0)(lambda: arrival(k, i).wait_recv())
-            pl.when(k < n - 1)(lambda: arrival(n, i).wait_recv())
-
-            def settle(b, carry):
-                here = pl.ds(pl.multiple_of(b * 2 * BLOCK, 2 * BLOCK), 2 * BLOCK)
-                for q in range(strips):
-                    low = slots[k, i, q, here].astype(jnp.float32)
-                    high = slots[n, i, q, here].astype(jnp.float32)
-                    value = slots[n + 1, i, q, here].astype(jnp.float32)
-                    value = value + jnp.where(k > 0, low, 0.0) + jnp.where(k < n - 1, high, 0.0)
-                    slots[n + 1, i, q, here] = value.astype(jnp.bfloat16)
+            for part in range(2):
+                pl.when(k > 0)(lambda: arrival(k, f, part).wait_recv())
+                pl.when(k < n - 1)(lambda: arrival(n, f, part).wait_recv())
+
+            def settle(q, carry):
+                for t in range(2):
+                    for row in range(2):
+                        here = pl.ds(pl.multiple_of(spot(t, row) * LANES, LANES), LANES)
+                        low = slots[k, f, q, here].astype(jnp.float32)
+                        high = slots[n, f, q, here].astype(jnp.float32)
+                        value = slots[n + 1, f, q, here].astype(jnp.float32)
+                        value = value + jnp.where(k > 0, low, 0.0) + jnp.where(k < n - 1, high, 0.0)
+                        exact = lax.dot_general(
+                            unit, value.astype(jnp.bfloat16), (((1,), (1,)), ((), ())),
+                            preferred_element_type=jnp.float32,
+                        )
+                        spaced[pl.ds(t * wide + row, LANES, stride=2), :] = exact
+                slots[n + 1, f, q] = spaced[pl.ds(0, 2 * wide), :].astype(jnp.bfloat16)
                 return carry
 
-            lax.fori_loop(0, wide // BLOCK, settle, 0)
-            keep(i).start()
-            give(i).start()
+            lax.fori_loop(0, strips, settle, 0)
+            keep(f).start()
+            give(f).start()
 
         return carry
 
-    lax.fori_loop(0, n * chunks, step, 0)
+    lax.fori_loop(0, steps, step, 0)
 
     def finish(i, carry):
         keep(i).wait()
@@ -411,7 +510,8 @@
         @pl.when(g != k)
         def _():
             def one(m, carry):
-                message(g, m).wait_send()
+                message(g, m, 0).wait_send()
+                message(g, m, 1).wait_send()
                 return carry
 
             lax.fori_loop(0, chunks, one, 0)
@@ -443,7 +543,7 @@
     width, most = stripes(velocities)
     total = chips * CORES
     wide = 2 * LANES
-    dist = distribution.transpose(0, 2, 3, 1).reshape(planes, wide, depth)
+    dist = distribution.reshape(planes, 2 * depth, LANES)
     fluid = jnp.broadcast_to((1 - cell_flags).astype(jnp.float32).reshape(1, wide), (8, wide))
     any_space = pl.BlockSpec(memory_space=pl.ANY)
     vmem = pl.BlockSpec(memory_space=pltpu.VMEM)
@@ -465,6 +565,8 @@
             pltpu.VMEM((chips + 2, most, width // LANES, 2 * wide, LANES), jnp.bfloat16),
             pltpu.VMEM((total, 8, wide), jnp.float32),
             pltpu.VMEM((total, wide, LANES), jnp.float32),
+            pltpu.VMEM((2, 2 * depth, LANES), jnp.bfloat16),
+            pltpu.VMEM((2 * depth, LANES), jnp.float32),
             dma((planes,)),
             dma((total,)), dma((total,)),
             dma((groups, planes)), dma((total,)),
@@ -473,7 +575,7 @@
             dma((most,)), dma((most,)),
             dma((total,)), dma((total,)),
             dma((2, 2)),
-            dma((chips, most)), dma((chips + 1, most)),
+            dma((2, chips, most)), dma((2, chips + 1, most)),
             dma((most,)), dma((most,)), dma((CORES * most,)),
         ],
         compiler_params=pltpu.CompilerParams(
@@ -481,7 +583,6 @@
         ),
         cost_estimate=pl.CostEstimate(flops=flops, bytes_accessed=velocities * depth * 2 * chips, transcendentals=0),
     )(dist, matrix, speeds, directions, fluid)
-    out = out.reshape(velocities // LANES, 2, LANES, LANES).transpose(0, 3, 1, 2)
     return out.reshape(1, velocities, 2, LANES)[:, : velocities - extra]
 
 

time: 311 us -> 287 us (0.923)
  local copies, waits for them, and re-layouts: 20.3 us -> 7.59 us
  Pallas kernels: 286 us -> 277 us
    transpose x2 -> x0, local copies, waits for them, and re-layouts: 19.7 us -> none  [the longest x1 9.88 us: on_device(): dist = distribution.transpose(0, 2, 3, 1).reshape(planes, wide, depth)]
    pallas_call x1, Pallas kernels: 286 us -> 277 us  [on_device(): pl.pallas_call(functools.partial(kernel, size), out_shape=(jax.ShapeDtype...]
    unnamed x0 -> x1, local copies, waits for them, and re-layouts: none -> 6.99 us
where the time goes in v3:
time: 287 us; the launch traced here: 285 us
  Pallas kernels  277 us (97%)
  local copies, waits for them, and re-layouts  7.59 us (3%)
    pallas_call x1, Pallas kernels, on_device(): pl.pallas_call(functools.partial(kernel, size), out_shape=(jax.ShapeDtype...  277 us
    unnamed x1, local copies, waits for them, and re-layouts  6.99 us

profile of v3, /device:TPU:8, one launch (start us, length us, event | category | flops | bytes accessed | tf_op | source)
XLA Modules:
  0.0 285.5 jit_solution(4378072726843490528)
XLA Ops:
  0.0 0.7 convert_bitcast_fusion
  0.7 0.6 broadcast_in_dim.8.fluid
  1.3 277.2 %shard_map.55 = (bf16[54,256,128]{2,1,0:T(8,128)(2,1)}, bf16[14,1728,256]{2,1,0:T(8,128)(2,1)}) custom-call(bf16[4,3456,128]{2,1,0:T(8,128)(2,1)} %bitcast.7, bf16[1728,6912]{1,0:T(8,128)(2,1)} %bitcast.6, f32[3,6912]{1,0:T(4,128)} %speeds.1, s32[3,6912]{1,0:T(4,128)} %directions.1, f32[8,256]{1,0:T(8,128)} %broadcast_in_dim.8.fluid), custom_call_target="tpu_custom_call" | custom-call | flops 122305904640 | bytes 95551488 | tf_op jit(solution)/shard_map/pallas_call | solution.py:553
  278.5 7.0 %copy.7 = bf16[1,6912,2,128]{3,2,1,0:T(2,128)(2,1)} copy(bf16[1,6912,2,128]{3,2,1,0:T(2,128)(2,1)} %bitcast.5) | data formatting | bytes 7077888

commit v4 on v3

--- a/solution.py
+++ b/solution.py
@@ -11,7 +11,8 @@
 CORES = 2
 LANES = 128
 BLOCK = 16
-KEPT = 2
+KEPT = 3
+AHEAD = 8
 
 
 def stripes(velocities):
@@ -61,24 +62,31 @@
     def turned(g):
         return jnp.where(mirror, n - 1 - g, g)
 
-    first_group = turned(jnp.where(at == 0, 1, 0)) if staged else 0
-    steps = (n + 1) * chunks if staged else n * chunks
+    first_group = turned(jnp.where(at <= 1, 1, 0)) if staged else 0
+    steps = n * chunks + AHEAD if staged else n * chunks
     last = steps - chunks
+
+    held_back = jnp.where(at == 0, KEPT, 0)
+    share = jnp.where(at == 0, 10, 12)
+    between = at == 1 if staged else False
+    begin = jnp.where(between, AHEAD, 0)
 
     def item(s):
         if not staged:
             return s // chunks, lax.rem(s, chunks)
-        j = s - 2 * chunks
-        third, rest = j // 3, lax.rem(j, 3)
-        sent = 2 * third + rest
-        length = jnp.where(at == 2, chunks, chunks - KEPT)
-        one, two = sent < length, sent < length + chunks
-        g = jnp.where(rest == 2, at, jnp.where(one | jnp.logical_not(two), jnp.where(at == 2, 1, 2), 3))
-        i = jnp.where(rest == 2, third, jnp.where(one, sent, jnp.where(two, sent - length, sent - chunks)))
+        j = s - AHEAD - chunks + held_back
+        done = jnp.minimum(share * j // 30, chunks)
+        alone = jnp.minimum(share * (j + 1) // 30, chunks) > done
+        sent = j - done
+        one, over = sent < chunks, sent >= 2 * chunks
+        g = jnp.where(one, jnp.where(at == 2, 1, 2), jnp.where(over, 1, 3))
+        i = jnp.where(one, sent, jnp.where(over, sent - chunks - KEPT, sent - chunks))
+        g = jnp.where(alone, jnp.where(at == 1, 0, at), g)
+        i = jnp.where(alone, done, i)
         g = jnp.where(final_chip, 1 + j // chunks, g)
-        i = jnp.where(final_chip, lax.rem(s, chunks), i)
+        i = jnp.where(final_chip, lax.rem(j, chunks), i)
         early = j < 0
-        return jnp.where(early, first_group, turned(g)), jnp.where(early, lax.rem(s, chunks), i)
+        return jnp.where(early, first_group, turned(g)), jnp.where(early, jnp.where(s < AHEAD, s, s - AHEAD), i)
 
     inner, outer = 1 - y, y
 
@@ -98,11 +106,20 @@
     def halo_of(p):
         return pl.ds(pl.multiple_of(total * wide + p * LANES, LANES), LANES)
 
-    def fetch(q):
-        return pltpu.make_async_copy(dist.at[q], raw.at[q % 2], l_sem.at[q])
-
-    def turn(q):
-        spaced[...] = raw[q % 2].astype(jnp.float32)
+    first_pair = lax.rem(first_group, planes // 2)
+
+    def halo_order(j):
+        if not staged:
+            return j
+        pair = first_pair if j < 2 else 1 - first_pair
+        return pair * 2 + j % 2
+
+    def fetch(j):
+        return pltpu.make_async_copy(dist.at[halo_order(j)], raw.at[j % 2], l_sem.at[j])
+
+    def turn(j):
+        q = halo_order(j)
+        spaced[...] = raw[j % 2].astype(jnp.float32)
         for row in range(2):
             values = spaced[pl.ds(row, depth, stride=2), :].astype(jnp.bfloat16)
             at = pl.ds(pl.multiple_of((x * planes + q) * wide + row * LANES, LANES), LANES)
@@ -129,6 +146,12 @@
         return remote(
             held.at[c, inner_of(p)], held.at[c, halo_of(p)], hs_sem.at[to, q], hr_sem.at[p],
             {"vout": to, "cell": 1 - y},
+        )
+
+    def relay(p):
+        to, q = p // planes, planes - 1 - lax.rem(p, planes)
+        return remote(
+            held.at[c, inner_of(p)], held.at[c, halo_of(p)], hs_sem.at[to, q], hr_sem.at[p], {"cell": 1 - y}
         )
 
     def halo_got(p):
@@ -171,34 +194,26 @@
             src, at = lent.at[i], 1 - c
         return pltpu.make_async_copy(src, tile.at[slot, at], t_sem.at[slot, which])
 
-    first_pair = lax.rem(first_group, planes // 2)
-
-    def halo_order(j):
-        if not staged:
-            return j
-        pair = first_pair if j < 2 else 1 - first_pair
-        return pair * 2 + j % 2
-
     def away(to, j):
         return jnp.where(x > to, j, planes - 1 - j)
 
     def from_group(src, j):
         return src * planes + jnp.where(src > x, j, planes - 1 - j)
 
-    load(0, 0).start()
-    for q in range(min(2, planes)):
-        fetch(q).start()
-    for q in range(planes):
-        fetch(q).wait()
-        turn(q)
-        if q + 2 < planes:
-            fetch(q + 2).start()
-        if q == 0:
+    load(begin, 0).start()
+    for j in range(min(2, planes)):
+        fetch(j).start()
+    for j in range(planes):
+        fetch(j).wait()
+        turn(j)
+        if j + 2 < planes:
+            fetch(j + 2).start()
+        if j == 0:
             pl.semaphore_wait(barrier, len(everyone))
             matrix_send(0).start()
-        core_own(q).start()
-    for j in range(min(2, planes)):
-        halo_send(x, halo_order(j)).start()
+        core_own(halo_order(j)).start()
+        if j < 2:
+            halo_send(x, halo_order(j)).start()
     for m in range(1, groups):
         to = other_group(m)
         main_send(to, away(to, 0)).start()
@@ -216,8 +231,9 @@
         to = other_group(m)
         for j in range(1, min(3, planes)):
             main_send(to, away(to, j)).start()
-        for j in range(min(2, planes)):
-            halo_send(to, away(to, j)).start()
+        if not staged:
+            for j in range(min(2, planes)):
+                halo_send(to, away(to, j)).start()
         for j in range(3, planes):
             main_send(to, away(to, j)).start()
         for j in range(2, planes):
@@ -226,7 +242,7 @@
     for q in range(strips):
         sums[q, 4 * wide : 5 * wide] = jnp.zeros((wide, LANES), jnp.float32)
     matrix_got(0).wait_recv()
-    load(0, 1).start()
+    load(begin, 1).start()
     for j in range(1, total):
         flag_got(j).wait_recv()
 
@@ -253,6 +269,10 @@
         for p in ps:
             main_got(p).wait_recv()
             core_pass(p).start()
+
+    def relay_rows(ps):
+        for p in ps:
+            relay(p).start()
 
     def end_main(ps):
         for p in ps:
@@ -271,14 +291,16 @@
                 for call, ps in calls:
                     call(ps)
 
-        when(chunks - 4, (pass_halo, own[:2]), (pass_main, near))
-        when(chunks, (end_halo, own[:2]), (end_main, near))
-        when(2 * chunks - 3, (pass_halo, own[2:]), (pass_main, middle))
-        when(2 * chunks, (end_halo, own[2:]))
-        when(2 * chunks - 1, (pass_halo, near_halo))
-        when(jnp.where(final_chip, 3 * chunks, 2 * chunks), (end_main, middle), (end_halo, near_halo))
-        when(2 * chunks + 12, (pass_main, far), (pass_halo, far_halo))
-        when(2 * chunks + 15, (end_main, far), (end_halo, far_halo))
+        when(jnp.where(between, AHEAD, AHEAD - 2), (pass_halo, own[:2]), (pass_main, near), (relay_rows, near))
+        when(AHEAD, (end_halo, own[:2]), (end_main, near))
+        when(AHEAD + 7, (pass_main, middle[:1]), (relay_rows, middle[:1]))
+        when(AHEAD + chunks - KEPT - 2, (pass_halo, own[2:]), (pass_main, middle[1:]), (pass_halo, near_halo))
+        when(AHEAD + chunks - KEPT, (end_halo, own[2:]))
+        when(
+            jnp.where(final_chip, AHEAD + 2 * chunks, AHEAD + chunks - KEPT), (end_main, middle), (end_halo, near_halo)
+        )
+        when(AHEAD + chunks + 12, (pass_main, far), (pass_halo, far_halo))
+        when(AHEAD + chunks + 15, (end_main, far), (end_halo, far_halo))
 
     if not staged:
         pass_halo(own)
@@ -339,9 +361,19 @@
 
         @pl.when(s + 1 < steps)
         def _():
-            @pl.when(s + 1 < chunks)
-            def _():
-                matrix_got(s + 1).wait_recv()
+            if staged:
+                later = s + 1 - AHEAD
+                first_use = jnp.where(between, 1, AHEAD)
+                pl.when(later < 0)(lambda: matrix_got(s + 1).wait_recv())
+                pl.when((later >= first_use) & (later < chunks - KEPT))(lambda: matrix_got(later).wait_recv())
+
+                @pl.when(later == chunks - KEPT)
+                def _():
+                    for e in range(KEPT):
+                        matrix_got(chunks - KEPT + e).wait_recv()
+
+            else:
+                pl.when(s + 1 < chunks)(lambda: matrix_got(s + 1).wait_recv())
 
             load(s + 1, 0).start()
             load(s + 1, 1).start()
@@ -357,7 +389,7 @@
             for q in range(strips):
                 sums[q, at : at + wide] = jnp.zeros((wide, LANES), jnp.float32)
 
-        full = s >= chunks if staged else s >= 0
+        full = s >= AHEAD if staged else s >= 0
 
         @pl.when(full)
         def _():
@@ -402,7 +434,7 @@
         through = ((g > k) & (k > 0)) | ((g < k) & (k < n - 1))
         into = jnp.where(g == k, n + 1, g)
         if staged:
-            does = (s < chunks) | (s >= 2 * chunks), s >= chunks
+            does = between | (s < AHEAD) | (g != first_group) | (i >= AHEAD), s >= AHEAD
         else:
             does = s >= 0, s >= 0
         for part in range(2):
@@ -460,10 +492,7 @@
         for part in range(2):
             pl.when((g != k) & does[part])(lambda: message(g, i, part).start())
 
-        f = s - last
-
-        @pl.when((f >= 0) & (f < chunks))
-        def _():
+        def conclude(f, carry):
             for part in range(2):
                 pl.when(k > 0)(lambda: arrival(k, f, part).wait_recv())
                 pl.when(k < n - 1)(lambda: arrival(n, f, part).wait_recv())
@@ -487,10 +516,16 @@
             lax.fori_loop(0, strips, settle, 0)
             keep(f).start()
             give(f).start()
+            return carry
+
+        behind = s - last - jnp.where(at == 1, KEPT, 0) if staged else s - last
+        low_end = jnp.maximum(behind, 0)
+        high_end = jnp.where(s == steps - 1, chunks, jnp.maximum(behind + 1, 0))
+        lax.fori_loop(low_end, high_end, conclude, 0)
 
         return carry
 
-    lax.fori_loop(0, steps, step, 0)
+    lax.fori_loop(begin, steps, step, 0)
 
     def finish(i, carry):
         keep(i).wait()

time: 287 us -> 281 us (0.979)
  the two profiles are of different devices: /device:TPU:8 before, /device:TPU:3 now
where the time goes in v4:
time: 281 us
  Pallas kernels  273 us (97%)
  local copies, waits for them, and re-layouts  7.59 us (3%)
    pallas_call x1, Pallas kernels, on_device(): pl.pallas_call(functools.partial(kernel, size), out_shape=(jax.ShapeDtype...  273 us
    unnamed x1, local copies, waits for them, and re-layouts  6.99 us

profile of v4, /device:TPU:3, one launch (start us, length us, event | category | flops | bytes accessed | tf_op | source)
XLA Modules:
  0.0 280.9 jit_solution(14076915379736709014)
XLA Ops:
  0.0 0.7 convert_bitcast_fusion
  0.7 0.6 broadcast_in_dim.8.fluid
  1.3 272.6 %shard_map.55 = (bf16[54,256,128]{2,1,0:T(8,128)(2,1)}, bf16[14,1728,256]{2,1,0:T(8,128)(2,1)}) custom-call(bf16[4,3456,128]{2,1,0:T(8,128)(2,1)} %bitcast.7, bf16[1728,6912]{1,0:T(8,128)(2,1)} %bitcast.6, f32[3,6912]{1,0:T(4,128)} %speeds.1, s32[3,6912]{1,0:T(4,128)} %directions.1, f32[8,256]{1,0:T(8,128)} %broadcast_in_dim.8.fluid), custom_call_target="tpu_custom_call" | custom-call | flops 122305904640 | bytes 95551488 | tf_op jit(solution)/shard_map/pallas_call | solution.py:588
  273.9 7.0 %copy.7 = bf16[1,6912,2,128]{3,2,1,0:T(2,128)(2,1)} copy(bf16[1,6912,2,128]{3,2,1,0:T(2,128)(2,1)} %bitcast.5) | data formatting | bytes 7077888

commit v5 on v4

--- a/solution.py
+++ b/solution.py
@@ -67,7 +67,7 @@
     last = steps - chunks
 
     held_back = jnp.where(at == 0, KEPT, 0)
-    share = jnp.where(at == 0, 10, 12)
+    share = jnp.where(at == 0, 10, jnp.where(at == 1, 10, 12))
     between = at == 1 if staged else False
     begin = jnp.where(between, AHEAD, 0)
 
@@ -518,7 +518,7 @@
             give(f).start()
             return carry
 
-        behind = s - last - jnp.where(at == 1, KEPT, 0) if staged else s - last
+        behind = s - last - jnp.where((at == 1) | (at == 2), KEPT, 0) if staged else s - last
         low_end = jnp.maximum(behind, 0)
         high_end = jnp.where(s == steps - 1, chunks, jnp.maximum(behind + 1, 0))
         lax.fori_loop(low_end, high_end, conclude, 0)

time: 281 us -> 281 us (level)
  the two profiles are of different devices: /device:TPU:3 before, /device:TPU:7 now
where the time goes in v5:
time: 281 us; the launch traced here: 280 us
  Pallas kernels  272 us (97%)
  local copies, waits for them, and re-layouts  7.59 us (3%)
    pallas_call x1, Pallas kernels, on_device(): pl.pallas_call(functools.partial(kernel, size), out_shape=(jax.ShapeDtype...  272 us
    unnamed x1, local copies, waits for them, and re-layouts  6.99 us

profile of v5, /device:TPU:7, one launch (start us, length us, event | category | flops | bytes accessed | tf_op | source)
XLA Modules:
  0.0 280.2 jit_solution(10279920334678459992)
XLA Ops:
  0.0 0.7 convert_bitcast_fusion
  0.7 0.6 broadcast_in_dim.8.fluid
  1.3 271.9 %shard_map.55 = (bf16[54,256,128]{2,1,0:T(8,128)(2,1)}, bf16[14,1728,256]{2,1,0:T(8,128)(2,1)}) custom-call(bf16[4,3456,128]{2,1,0:T(8,128)(2,1)} %bitcast.7, bf16[1728,6912]{1,0:T(8,128)(2,1)} %bitcast.6, f32[3,6912]{1,0:T(4,128)} %speeds.1, s32[3,6912]{1,0:T(4,128)} %directions.1, f32[8,256]{1,0:T(8,128)} %broadcast_in_dim.8.fluid), custom_call_target="tpu_custom_call" | custom-call | flops 122305904640 | bytes 95551488 | tf_op jit(solution)/shard_map/pallas_call | solution.py:588
  273.2 7.0 %copy.7 = bf16[1,6912,2,128]{3,2,1,0:T(2,128)(2,1)} copy(bf16[1,6912,2,128]{3,2,1,0:T(2,128)(2,1)} %bitcast.5) | data formatting | bytes 7077888
